TPU v7x, 128 devices: a whole 4x4x4 slice. The times are simulated.
128 devices in a mesh: edge: 8 (over x, y_lo), feat: 16 (over z, y_hi, core).
Axes of the slice: x: 4, y: 4 (y_hi: 2, y_lo: 2; y = y_hi * 2 + y_lo), z: 4, core: 2. Of those that a mesh axis runs over, the one named last changes fastest.
Arguments:
- grad_out: bfloat16 [262144, 256], P(('edge', 'feat')), may hold values from -6 to 6
- pre_act: bfloat16 [262144, 256], P(('edge', 'feat')), may hold values from -6 to 6
- feat_t: bfloat16 [128, 262144], P('feat', 'edge'), may hold values from -6 to 6
- agg_t: bfloat16 [128, 262144], P('feat', 'edge'), may hold values from -6 to 6
- w_self: bfloat16 [128, 256], replicated, may hold values from -0.375 to 0.375
- w_neigh: bfloat16 [128, 256], replicated, may hold values from -0.375 to 0.375
- blocks: bfloat16 [16384, 4096], P('edge'), may hold values from 0 to 0.029907227
- row_index: int32 [16384], P('edge'), may hold values from 0 to 511, as said below
- col_index: int32 [16384], P('edge'), may hold values from 0 to 4095
- counts: int32 [8], P('edge'), may hold values from 512 to 2048, as said below
Outputs:
- grad_feat_t: bfloat16 [128, 262144], P('feat', 'edge')
- grad_w_self: float32 [128, 256], P('feat')
- grad_w_neigh: float32 [128, 256], P('feat')
Inputs may be any that keep to these rules, and one draw needn't show every extreme that they name: `counts`: slots at or after a partition's count hold arbitrary indices and values and are ignored; some partition is full in every draw. `row_index`: indices are local to the slab of the slot's partition.
All inputs are finite; a program needn't handle non-finite values.
Results may differ from a plain program's by a relative error of at most 0.0075.
Values may be sent and summed in bfloat16 or wider, within the bound.
A program may use at most 192 MiB of HBM per device.

v0:
```python
import math

import jax
import jax.numpy as jnp
from jax import lax
from jax.sharding import PartitionSpec as P


def spread_slots(node_rows, blocks, row_index, col_index, live_count, slot_count, totals):
    feat_local = node_rows.shape[1] // 64
    values = blocks.reshape(slot_count, 64, 64)
    gathered = jnp.take(node_rows, row_index, axis=0).reshape(slot_count, feat_local, 64)
    product = jnp.einsum("sfi,sij->sfj", gathered, values, preferred_element_type=jnp.float32)
    product = product.reshape(slot_count, feat_local * 64)
    slot_ids = jnp.arange(slot_count, dtype=jnp.int32)
    product = jnp.where((slot_ids < live_count)[:, None], product, jnp.float32(0.0))
    return totals.at[col_index].add(product)


def on_device(
    grad_out, pre_act, feat_t, agg_t, w_self, w_neigh, blocks, row_index, col_index, counts
):
    feat_local = feat_t.shape[0]
    slab_nodes = feat_t.shape[1]
    all_nodes = slab_nodes * lax.axis_size("edge")
    factor = 1.0 / math.sqrt(all_nodes)
    masked = jnp.where(pre_act > 0, grad_out, jnp.zeros_like(grad_out))
    stacked = jnp.stack([w_self, w_neigh])
    backs = jnp.einsum("wfh,rh->wfr", stacked, masked, preferred_element_type=jnp.float32).astype(
        jnp.bfloat16
    )
    moved = lax.all_to_all(backs, "feat", split_axis=1, concat_axis=2, tiled=True)
    piece = lax.all_gather(masked, "feat", axis=0, tiled=True)
    part_self = jnp.dot(feat_t, piece, preferred_element_type=jnp.float32)
    part_neigh = jnp.dot(agg_t, piece, preferred_element_type=jnp.float32)
    sum_self, sum_neigh = lax.psum((part_self, part_neigh), "edge")
    grad_w_self = sum_self * factor
    grad_w_neigh = sum_neigh * factor
    node_rows = (
        moved[1]
        .reshape(feat_local, slab_nodes // 64, 64)
        .transpose(1, 0, 2)
        .reshape(slab_nodes // 64, feat_local * 64)
    )
    live_count = counts[0]
    slot_total = blocks.shape[0]
    column_blocks = all_nodes // 64
    totals = jnp.zeros((column_blocks, feat_local * 64), jnp.float32)
    totals = spread_slots(node_rows, blocks, row_index, col_index, live_count, slot_total, totals)
    received = lax.psum_scatter(
        totals.astype(jnp.bfloat16), "edge", scatter_dimension=0, tiled=True
    ).astype(jnp.float32)
    spread = (
        received.reshape(slab_nodes // 64, feat_local, 64)
        .transpose(1, 0, 2)
        .reshape(feat_local, slab_nodes)
    )
    grad_feat_t = (moved[0].astype(jnp.float32) + spread).astype(jnp.bfloat16)
    return (grad_feat_t, grad_w_self, grad_w_neigh)


def solution(mesh):
    in_specs = (
        P(("edge", "feat"), None),
        P(("edge", "feat"), None),
        P("feat", "edge"),
        P("feat", "edge"),
        P(),
        P(),
        P("edge", None),
        P("edge"),
        P("edge"),
        P("edge"),
    )
    out_specs = (P("feat", "edge"), P("feat", None), P("feat", None))
    return jax.shard_map(
        on_device, mesh=mesh, in_specs=in_specs, out_specs=out_specs, check_vma=False
    )
```

profile of v0, /device:TPU:0, one launch (start us, length us, event | category | flops | bytes accessed | tf_op | source)
XLA Modules:
  0.0 378.8 jit_solution(16462164012486771464)
XLA Ops:
  8.0 0.0 copy-start
  8.0 1.7 compare_select_fusion
  9.7 0.0 copy-start.2
  9.7 1.5 convolution_convert_fusion
  11.2 2.1 copy.33
  13.3 8.1 %all-to-all-start = ((bf16[2,128,2048]{2,0,1:T(2,128)(2,1)}), bf16[2,128,2048]{2,0,1:T(2,128)(2,1)S(1)}, u32[]{:S(2)}, u32[]{:S(2)}) async-start(bf16[2,128,2048]{2,0,1:T(2,128)(2,1)} %copy.33), calls=%async_computation | async-start | bytes 2097152 | tf_op jit(solution)/shard_map/all_to_all | solution.py:32
  21.5 0.0 reduce-scatter.2.cloned.1.call-start
  21.5 22.6 %copy.38 = bf16[2048,4096]{0,1:T(8,128)(2,1)} copy(bf16[2048,4096]{1,0:T(8,128)(2,1)} %param.16) | data formatting | bytes 33554432 | tf_op args[6]
  44.1 0.0 copy-done.2
  44.1 0.0 copy-start.5
  44.1 0.0 copy-start.6
  44.1 45.9 %copy.40 = bf16[2048,64,64]{2,1,0:T(8,128)(2,1)} copy(bf16[2048,64,64]{0,2,1:T(8,128)(2,1)} %bitcast.36) | data formatting | bytes 33554432 | tf_op jit(solution)/shard_map/reshape | solution.py:11
  90.7 0.0 copy-done.5
  90.7 0.0 copy-done.6
  90.8 0.0 all-to-all-done
  90.8 0.6 copy.47
  91.4 1.1 fusion.8
  92.5 1.1 reshape_squeeze.3
  93.6 0.3 copy.35
  93.9 0.2 copy.36
  94.1 7.5 %gather_fusion = bf16[2048,512]{1,0:T(8,128)(2,1)S(1)} fusion(bf16[512,512]{1,0:T(8,128)(2,1)S(1)} %copy.36, s32[2048]{0:T(1024)S(1)} %fusion.6), kind=kCustom, calls=%fused_computation | custom fusion | bytes 4202496 | tf_op jit(solution)/shard_map/jit(_take)/gather | solution.py:12
  101.7 2.5 copy.37
  104.2 1.8 broadcast_select_fusion
  106.0 4.3 %copy.39 = bf16[2048,8,64]{2,1,0:T(8,128)(2,1)} copy(bf16[2048,8,64]{0,2,1:T(8,128)(2,1)S(1)} %broadcast_select_fusion) | data formatting | bytes 4194304 | tf_op jit(solution)/shard_map/jit(_take)/select_n | solution.py:12
  110.3 18.2 %fusion.9 = f32[2048,8,64]{2,1,0:T(8,128)} fusion(bf16[2048,8,64]{2,1,0:T(8,128)(2,1)} %copy.39, bf16[2048,64,64]{2,1,0:T(8,128)(2,1)} %copy.40), kind=kOutput, calls=%fused_computation.26 | convolution fusion | flops 134217728 | bytes 23068672 | tf_op jit(solution)/shard_map/sfi,sij->sfj/dot_general | solution.py:13
  128.5 6.9 %copy.41 = f32[2048,8,64]{0,2,1:T(8,128)} copy(f32[2048,8,64]{2,1,0:T(8,128)} %fusion.9) | data formatting | bytes 8388608 | tf_op jit(solution)/shard_map/sfi,sij->sfj/dot_general | solution.py:13
  135.4 4.8 %bitcast_select_fusion = f32[2048,512]{0,1:T(8,128)} fusion(f32[2048,8,64]{0,2,1:T(8,128)} %copy.41, pred[2048]{0:T(1024)(128)(4,1)S(1)} %iota_compare_fusion), kind=kLoop, calls=%fused_computation.2 | loop fusion | flops 1048576 | bytes 8390656 | tf_op jit(solution)/shard_map/jit(_where)/select_n | solution.py:16
  140.1 5.4 %copy.42 = f32[2048,512]{1,0:T(8,128)} copy(f32[2048,512]{0,1:T(8,128)} %bitcast_select_fusion) | data formatting | bytes 8388608 | tf_op jit(solution)/shard_map/jit(_where)/select_n | solution.py:16
  145.5 17.1 %scatter_custom_fusion = f32[4096,512]{1,0:T(8,128)} fusion(s32[2048]{0:T(1024)S(1)} %compare_select_fusion.2, f32[2048,512]{1,0:T(8,128)} %copy.42, f32[]{:T(128)} %constant.9.clone.1), kind=kCustom, calls=%fused_computation.3 | custom fusion | flops 1048576 | bytes 8389120 | tf_op jit(solution)/shard_map/scatter-add | solution.py:17
  162.7 5.9 %convert_element_type.19 = bf16[4096,512]{1,0:T(8,128)(2,1)} convert(f32[4096,512]{1,0:T(8,128)} %scatter_custom_fusion) | non-fusion elementwise | flops 2097152 | bytes 12582912 | tf_op jit(solution)/shard_map/convert_element_type | solution.py:51
  168.5 0.0 copy-start.3
  168.5 0.0 reduce-scatter.2.cloned.1.call-update
  168.5 0.0 all-gather.2.cloned.1.call-start
  168.6 0.5 all-gather.2.cloned.1.call-update
  169.1 0.6 copy-done.3
  169.7 1.6 copy.45
  171.3 145.3 %reduce-scatter.2.cloned.1.call-done = bf16[512,512]{1,0:T(8,128)(2,1)} async-done(((bf16[4096,512]{1,0:T(8,128)(2,1)}), bf16[512,512]{1,0:T(8,128)(2,1)}) %reduce-scatter.2.cloned.1.call-update) | async-done | bytes 524304 | tf_op jit(solution)/shard_map/reduce_scatter | solution.py:50
  316.6 2.2 copy.43
  318.9 1.8 copy.44
  320.7 1.6 reshape.55
  322.3 2.4 add_convert_fusion
  324.8 0.0 copy-done
  324.8 8.2 %convolution_bitcast_fusion = f32[8,256]{1,0:T(8,128)S(1)} fusion(bf16[32768,256]{1,0:T(8,128)(2,1)} %all-gather.2.cloned.1.call-done, bf16[8,32768]{1,0:T(8,128)(2,1)S(1)} %copy-done), kind=kOutput, calls=%fused_computation.8 | convolution fusion | flops 134217728 | bytes 17309696 | tf_op jit(solution)/shard_map/dot_general | solution.py:35
  333.0 0.0 copy-done.4
  333.0 2.5 copy-done.1
  335.5 2.3 convolution_bitcast_fusion.1
  337.8 32.9 %all-reduce = (f32[8,256]{1,0:T(8,128)S(1)}, f32[8,256]{1,0:T(8,128)S(1)}) all-reduce(f32[8,256]{1,0:T(8,128)S(1)} %convolution_bitcast_fusion.1, f32[8,256]{1,0:T(8,128)S(1)} %convolution_bitcast_fusion), channel_id=1, replica_groups=mesh['edge'=8,'feat'=16] {'edge'}, use_global_device_ids=true, to_apply=%region_2.3 | all-reduce | flops 4096 | bytes 32768 | tf_op jit(solution)/shard_map/psum | solution.py:36
  370.7 0.6 broadcast_multiply_fusion
  (7 shorter events, 0.0 us)
Async XLA Ops:
  8.0 316.8 %copy-start = (bf16[8,32768]{1,0:T(8,128)(2,1)S(1)}, bf16[8,32768]{1,0:T(8,128)(2,1)}, u32[]{:S(2)}) copy-start(bf16[8,32768]{1,0:T(8,128)(2,1)} %param.13) | copy-start | bytes 1572868
  9.7 34.4 %copy-start.2 = (bf16[2048,256]{1,0:T(8,128)(2,1)}, bf16[2048,256]{1,0:T(8,128)(2,1)S(1)}, u32[]{:S(2)}) copy-start(bf16[2048,256]{1,0:T(8,128)(2,1)S(1)} %compare_select_fusion) | copy-start | bytes 3145732
  13.3 77.4 %all-to-all-start = ((bf16[2,128,2048]{2,0,1:T(2,128)(2,1)}), bf16[2,128,2048]{2,0,1:T(2,128)(2,1)S(1)}, u32[]{:S(2)}, u32[]{:S(2)}) async-start(bf16[2,128,2048]{2,0,1:T(2,128)(2,1)} %copy.33), calls=%async_computation | async-start | bytes 2097152 | tf_op jit(solution)/shard_map/all_to_all | solution.py:32
  21.5 295.2 %reduce-scatter.2.cloned.1.call-start = ((), (), s32[]{:S(2)}) async-start(), calls=%async_computation.2 | async-start | bytes 4718592 | tf_op jit(solution)/shard_map/reduce_scatter | solution.py:50
  44.1 46.6 %copy-start.5 = (s32[2048]{0:T(1024)S(1)}, s32[2048]{0:T(1024)}, u32[]{:S(2)}) copy-start(s32[2048]{0:T(1024)} %param.17) | copy-start | bytes 24580
  44.1 46.6 %copy-start.6 = (s32[2048]{0:T(1024)S(1)}, s32[2048]{0:T(1024)}, u32[]{:S(2)}) copy-start(s32[2048]{0:T(1024)} %param.18) | copy-start | bytes 24580
  168.5 1.2 copy-start.3
  168.5 156.2 %all-gather.2.cloned.1.call-start = ((), (), s32[]{:S(2)}) async-start(), calls=%async_computation.3 | async-start | bytes 17825792 | tf_op jit(solution)/shard_map/all_gather | solution.py:33
  324.8 8.2 %copy-start.4 = (bf16[8,32768]{1,0:T(8,128)(2,1)S(1)}, bf16[8,32768]{1,0:T(8,128)(2,1)}, u32[]{:S(2)}) copy-start(bf16[8,32768]{1,0:T(8,128)(2,1)} %param.12) | copy-start | bytes 1572868
  324.8 10.7 %copy-start.1 = (bf16[32768,256]{1,0:T(8,128)(2,1)S(1)}, bf16[32768,256]{1,0:T(8,128)(2,1)}, u32[]{:S(2)}) copy-start(bf16[32768,256]{1,0:T(8,128)(2,1)} %all-gather.2.cloned.1.call-done) | copy-start | bytes 50331652
Sparse Core Ops, SparseCore 0:
  168.7 147.9 reduce-scatter.1
Sparse Core Ops, SparseCore 1:
  171.5 132.5 all-gather.1
where the time goes:
time: 381 us; the launch traced here: 379 us
  waiting for transfers between devices  146 us (38%)
  local copies, waits for them, and re-layouts  110 us (29%)
  other arithmetic  35.4 us (9%)
  blocking collectives  32.9 us (9%)
  matrix products  30.1 us (8%)
  between operations  16.3 us (4%)
  starting transfers between devices  8.22 us (2%)
    reduce_scatter x1, waiting for transfers between devices, on_device(): lax.psum_scatter(totals.astype(jnp.bfloat16), 'edge', scatter_dimension=0...  145 us
    reshape x1, local copies, waits for them, and re-layouts, spread_slots(): values = blocks.reshape(slot_count, 64, 64)  45.9 us
    psum x1, blocking collectives, on_device(): sum_self, sum_neigh = lax.psum((part_self, part_neigh), 'edge')  32.9 us
    unnamed x16, local copies, waits for them, and re-layouts  27.3 us
    dot_general x1, matrix products, spread_slots(): jnp.einsum('sfi,sij->sfj', gathered, values, preferred_element_type=jnp.f...  18.2 us
    scatter-add x1, other arithmetic, spread_slots(): return totals.at[col_index].add(product)  17.1 us
    gather x2, local copies, waits for them, and re-layouts, spread_slots(): jnp.take(node_rows, row_index, axis=0).reshape(slot_count, feat_local, 64)  10.1 us
    dot_general x1, matrix products, on_device(): part_neigh = jnp.dot(agg_t, piece, preferred_element_type=jnp.float32)  8.18 us
  transfers between devices with their start and end apart: 3, of which 1 were waited for; matrix products, arithmetic and copies ran while one was open for 21% of the time, Pallas kernels for 0%

commit v1 on v0

v1 whole, which is shorter than its diff:
```python
import functools
import math

import jax
import jax.numpy as jnp
from jax import lax
from jax.experimental import pallas as pl
from jax.experimental.pallas import tpu as pltpu
from jax.sharding import PartitionSpec as P

MESH = pl.DeviceIdType.MESH
MIB = 2**20
F32 = jnp.float32
BF16 = jnp.bfloat16
HIGH = dict(preferred_element_type=F32)
NT = (((1,), (1,)), ((), ()))


def masked_rows(grad_ref, pre_ref):
    return jnp.where(pre_ref[...] > 0, grad_ref[...], jnp.zeros_like(grad_ref))


def halves_of(product, owner, out_ref):
    nodes = product.shape[1]
    rows = product[owner * 8 : owner * 8 + 8]
    both = jnp.concatenate([rows[:, : nodes // 2], rows[:, nodes // 2 :]], 0)
    out_ref[owner] = both.astype(BF16)


def neigh_kernel(n_feat, grad_ref, pre_ref, w_ref, out_ref, send, masked, send_sem, recv_sem, own_sem):
    me = lax.axis_index("feat")
    barrier = pltpu.get_barrier_semaphore()
    for k in range(1, n_feat):
        peer = lax.rem(me + k, n_feat)
        pl.semaphore_signal(barrier, inc=1, device_id={"feat": peer}, device_id_type=MESH)

    masked[...] = masked_rows(grad_ref, pre_ref)
    product = lax.dot_general(w_ref[...], masked[...], NT, **HIGH)
    for owner in range(n_feat):
        halves_of(product, owner, send)

    own = pltpu.make_async_copy(send.at[me], out_ref.at[me], own_sem)
    own.start()
    pl.semaphore_wait(barrier, n_feat - 1)

    def copy(peer, slot):
        return pltpu.make_async_remote_copy(
            src_ref=send.at[peer],
            dst_ref=out_ref.at[slot],
            send_sem=send_sem.at[peer],
            recv_sem=recv_sem.at[slot],
            device_id={"feat": peer},
            device_id_type=MESH,
        )

    for k in range(1, n_feat):
        copy(lax.rem(me + k, n_feat), me).start()
    for k in range(1, n_feat):
        copy(lax.rem(me + k, n_feat), me).wait_send()
    for k in range(1, n_feat):
        peer = lax.rem(me + k, n_feat)
        copy(peer, peer).wait_recv()
    own.wait()


def send_neigh(grad_out, pre_act, w_neigh, n_feat):
    nodes, hidden = grad_out.shape
    return pl.pallas_call(
        functools.partial(neigh_kernel, n_feat),
        in_specs=[pl.BlockSpec(memory_space=pltpu.VMEM)] * 3,
        out_specs=pl.BlockSpec(memory_space=pl.ANY),
        out_shape=jax.ShapeDtypeStruct((n_feat, 16, nodes // 2), BF16),
        scratch_shapes=[
            pltpu.VMEM((n_feat, 16, nodes // 2), BF16),
            pltpu.VMEM((nodes, hidden), BF16),
            pltpu.SemaphoreType.DMA((n_feat,)),
            pltpu.SemaphoreType.DMA((n_feat,)),
            pltpu.SemaphoreType.DMA,
        ],
        compiler_params=pltpu.CompilerParams(
            collective_id=0, has_side_effects=True, vmem_limit_bytes=48 * MIB
        ),
        name="send_neigh",
    )(grad_out, pre_act, w_neigh)


def spread_kernel(
    per_step, counts_ref, row_ref, col_ref, neigh_hbm, blocks_hbm, out_hbm,
    neigh, blocks, table, totals, even, odd, packed, neigh_sem, block_sem, out_sem,
):
    steps = blocks.shape[0] // per_step
    pairs = totals.shape[0] - 1
    n_src, _, span = neigh.shape
    n_dest = packed.shape[0]

    def load(i):
        rows = pl.ds(i * per_step, per_step)
        return pltpu.make_async_copy(blocks_hbm.at[rows], blocks.at[rows], block_sem.at[i])

    load_neigh = pltpu.make_async_copy(neigh_hbm, neigh, neigh_sem)
    load_neigh.start()
    for i in range(steps):
        load(i).start()

    @pl.loop(0, pairs // 64)
    def _(i):
        totals[pl.ds(i * 64, 64)] = jnp.zeros((64, 8, 128), F32)

    totals[pairs] = jnp.zeros((8, 128), F32)

    place = lax.broadcasted_iota(jnp.int32, (128, 2048), 1)
    source = place // 1024 * 64 + (place % 512) // 16 * 2 + place // 512 % 2
    node = lax.broadcasted_iota(jnp.int32, (128, 2048), 0)
    permute = jnp.where(source == node, 1.0, 0.0).astype(BF16)
    load_neigh.wait()
    tiles = span // 128

    @pl.loop(0, n_src)
    def _(src):
        x = jnp.concatenate([neigh[src, :, t * 128 : (t + 1) * 128] for t in range(tiles)], 0)
        for b in range(2):
            y = jnp.dot(x, permute[:, b * 1024 : (b + 1) * 1024], **HIGH)
            for t in range(tiles):
                for h in range(2):
                    at = t * 16 + h * 8
                    both = jnp.concatenate([y[at : at + 8, :512], y[at : at + 8, 512:]], 0)
                    table[src * (4 * tiles) + h * 2 * tiles + 2 * t + b] = both.astype(BF16)

    lane = lax.broadcasted_iota(jnp.int32, (8, 128), 1)
    own = lax.broadcasted_iota(jnp.int32, (16, 512), 1) % 16

    @pl.loop(0, steps)
    def _(step):
        first = step * per_step
        live = counts_ref[0] - first
        load(step).wait()

        def product(g, dst):
            left = []
            for q in range(16):
                s = g * 16 + q
                r = jnp.where(s < live, row_ref[first + s], 0)
                left.append(jnp.where(own == q, table[r], jnp.zeros((16, 512), BF16)))
            rows = pl.ds(pl.multiple_of(first + g * 16, 16), 16)
            right = jnp.concatenate([blocks[rows, t * 128 : (t + 1) * 128] for t in range(32)], 0)
            dst[...] = jnp.dot(jnp.concatenate(left, 0), right, **HIGH)

        def collect(g, src):
            for q in range(16):
                s = g * 16 + q
                c = jnp.where(s < live, col_ref[first + s], 2 * pairs)
                v = jnp.where(lane < 64, src[q * 16 : q * 16 + 8], src[q * 16 + 8 : q * 16 + 16])
                v = v + pltpu.roll(v, 64, 1)
                totals[c // 2] += jnp.where(lane // 64 == c % 2, v, 0.0)

        @pl.when(live > 0)
        def _():
            n = per_step // 16
            kept = (even, odd)
            product(0, even)
            for g in range(1, n):
                product(g, kept[g % 2])
                collect(g - 1, kept[(g - 1) % 2])
            collect(n - 1, kept[(n - 1) % 2])

    per = pairs // n_dest
    half = per // 2

    def store(e):
        return pltpu.make_async_copy(packed.at[e], out_hbm.at[e], out_sem.at[e])

    @pl.loop(0, n_dest)
    def _(e):
        @pl.loop(0, half // 16)
        def _(k):
            for u in range(16):
                at = k * 16 + u
                both = jnp.concatenate([totals[e * per + at], totals[e * per + half + at]], 0)
                packed[e, :, pl.ds(pl.multiple_of(at * 128, 128), 128)] = both.astype(BF16)

        store(e).start()

    @pl.loop(0, n_dest)
    def _(e):
        store(e).wait()


def spread_slots(counts, row_index, col_index, neigh, blocks, n_dest, slab_nodes):
    slots = blocks.shape[0]
    per_step = 128
    pairs = n_dest * slab_nodes // 128
    smem = pl.BlockSpec(memory_space=pltpu.SMEM)
    hbm = pl.BlockSpec(memory_space=pl.ANY)
    return pl.pallas_call(
        functools.partial(spread_kernel, per_step),
        in_specs=[smem, smem, smem, hbm, hbm],
        out_specs=hbm,
        out_shape=jax.ShapeDtypeStruct((n_dest, 16, slab_nodes // 2), BF16),
        scratch_shapes=[
            pltpu.VMEM(neigh.shape, BF16),
            pltpu.VMEM(blocks.shape, BF16),
            pltpu.VMEM((slab_nodes // 64, 16, 512), BF16),
            pltpu.VMEM((pairs + 1, 8, 128), F32),
            pltpu.VMEM((256, 128), F32),
            pltpu.VMEM((256, 128), F32),
            pltpu.VMEM((n_dest, 16, slab_nodes // 2), BF16),
            pltpu.SemaphoreType.DMA,
            pltpu.SemaphoreType.DMA((slots // per_step,)),
            pltpu.SemaphoreType.DMA((n_dest,)),
        ],
        compiler_params=pltpu.CompilerParams(vmem_limit_bytes=56 * MIB),
        name="spread_slots",
    )(counts, row_index, col_index, neigh, blocks)


def finish_kernel(
    n_feat, factor, grad_ref, pre_ref, w_ref, feat_ref, agg_ref, totals_hbm,
    out_ref, grad_self_ref, grad_neigh_ref,
    masked, back_send, back_recv, node_send, node_recv, terms, terms_recv, term, edge_recv,
    own, mine, one_recv, two_recv, three_send, three_recv, y_send, y_recv,
    back_ss, back_rs, node_ss, node_rs, term_ss, term_rs, edge_ss, edge_rs,
    load_sem, one_ss, one_rs, two_ss, two_rs, three_ss, three_rs, y_ss, y_rs,
):
    f = lax.axis_index("feat")
    e = lax.axis_index("edge")
    x, y = e // 2, e % 2
    n_edge = 8
    barrier = pltpu.get_barrier_semaphore()
    for k in range(1, n_feat):
        peer = {"feat": lax.rem(f + k, n_feat)}
        pl.semaphore_signal(barrier, inc=1, device_id=peer, device_id_type=MESH)
    for k in range(1, n_edge):
        peer = {"edge": lax.rem(e + k, n_edge)}
        pl.semaphore_signal(barrier, inc=1, device_id=peer, device_id_type=MESH)

    lanes = totals_hbm.shape[2] // 4

    def sub(j):
        return pl.ds(j * lanes, lanes)

    def edge_at(dx, py):
        return lax.rem(x + dx + 4, 4) * 2 + py

    def y_of(phase):
        return 1 - y if phase == 0 else y

    step_of = (1, -1)
    loads = []
    for phase in range(2):
        loads.append(
            pltpu.make_async_copy(totals_hbm.at[edge_at(0, y_of(phase))], own.at[phase], load_sem.at[3 * phase])
        )
        for d in range(2):
            loads.append(
                pltpu.make_async_copy(
                    totals_hbm.at[edge_at(step_of[d], y_of(phase)), :, pl.ds(d * 2 * lanes, 2 * lanes)],
                    mine.at[phase, d],
                    load_sem.at[3 * phase + 1 + d],
                )
            )
    for c in loads:
        c.start()

    def edge_copy(src, dst, send_sem, recv_sem, d):
        return pltpu.make_async_remote_copy(
            src_ref=src, dst_ref=dst, send_sem=send_sem, recv_sem=recv_sem,
            device_id={"edge": edge_at(step_of[d], y)}, device_id_type=MESH,
        )

    def one(p, d, j):
        src = totals_hbm.at[edge_at(2, y_of(p)), :, sub(2 * d + j)]
        return edge_copy(src, one_recv.at[p, d, j], one_ss.at[p, d, j], one_rs.at[p, d, j], d)

    def two(p, d, j):
        src = totals_hbm.at[edge_at(step_of[d], y_of(p)), :, sub(2 * (1 - d) + j)]
        return edge_copy(src, two_recv.at[p, d, j], two_ss.at[p, d, j], two_rs.at[p, d, j], d)

    def three(p, d, j):
        return edge_copy(
            three_send.at[p, d, j], three_recv.at[p, d, j], three_ss.at[p, d, j], three_rs.at[p, d, j], d
        )

    def y_copy(j):
        return pltpu.make_async_remote_copy(
            src_ref=y_send.at[j], dst_ref=y_recv.at[j], send_sem=y_ss.at[j], recv_sem=y_rs.at[j],
            device_id={"edge": edge_at(0, 1 - y)}, device_id_type=MESH,
        )

    def feat_copy(src, dst, send_sem, recv_sem, peer, slot):
        return pltpu.make_async_remote_copy(
            src_ref=src.at[peer], dst_ref=dst.at[slot], send_sem=send_sem.at[peer], recv_sem=recv_sem.at[slot],
            device_id={"feat": peer}, device_id_type=MESH,
        )

    def back_copy(peer, slot):
        return feat_copy(back_send, back_recv, back_ss, back_rs, peer, slot)

    def node_copy(peer, slot):
        return feat_copy(node_send, node_recv, node_ss, node_rs, peer, slot)

    def term_copy(peer, slot):
        return feat_copy(terms, terms_recv, term_ss, term_rs, peer, slot)

    def edge_term(peer, slot):
        return pltpu.make_async_remote_copy(
            src_ref=term, dst_ref=edge_recv.at[slot], send_sem=edge_ss.at[peer], recv_sem=edge_rs.at[slot],
            device_id={"edge": peer}, device_id_type=MESH,
        )

    def feat_peers():
        return [lax.rem(f + k, n_feat) for k in range(1, n_feat)]

    def edge_peers():
        return [lax.rem(e + k, n_edge) for k in range(1, n_edge)]

    pl.semaphore_wait(barrier, n_feat - 1 + n_edge - 1)
    for j in range(2):
        for d in range(2):
            one(0, d, j).start()
    for j in range(2):
        for d in range(2):
            two(0, d, j).start()

    nodes = grad_ref.shape[0]

    for owner in range(n_feat):
        span = slice(owner * nodes, (owner + 1) * nodes)
        both = jnp.concatenate([feat_ref[:, span].astype(F32), agg_ref[:, span].astype(F32)], 0)
        node_send[owner] = both.astype(BF16)
    for peer in feat_peers():
        node_copy(peer, f).start()
    masked[...] = masked_rows(grad_ref, pre_ref)
    product = lax.dot_general(w_ref[...], masked[...], NT, **HIGH)
    for owner in range(n_feat):
        halves_of(product, owner, back_send)
    for peer in feat_peers():
        back_copy(peer, f).start()
    node_recv[f] = node_send[f]
    back_recv[f] = back_send[f]
    for c in loads:
        c.wait()

    def relay(p):
        for j in range(2):
            for d in range(2):
                one(p, d, j).wait_recv()
                at = slice(j * lanes, (j + 1) * lanes)
                total = mine[p, d, :, at].astype(F32) + one_recv[p, d, j].astype(F32)
                three_send[p, d, j] = total.astype(BF16)
                three(p, d, j).start()

    def arrived(p, half, j):
        at = slice((2 * half + j) * lanes, (2 * half + j + 1) * lanes)
        return (
            own[p, :, at].astype(F32)
            + three_recv[p, half, j].astype(F32)
            + two_recv[p, 1 - half, j].astype(F32)
        )

    relay(0)
    for j in range(2):
        for d in range(2):
            one(1, d, j).start()
    for j in range(2):
        for d in range(2):
            two(1, d, j).start()

    for peer in feat_peers():
        node_copy(peer, peer).wait_recv()
    stacked = node_recv[...].reshape(n_feat * 16, nodes)
    partial = jnp.dot(stacked, masked[...], **HIGH)
    terms[...] = partial.reshape(terms.shape)
    for peer in feat_peers():
        term_copy(peer, f).start()

    for j in range(2):
        for half in range(2):
            two(0, 1 - half, j).wait_recv()
            three(0, half, j).wait_recv()
            y_send[2 * half + j] = arrived(0, half, j).astype(BF16)
            y_copy(2 * half + j).start()

    terms_recv[f] = terms[f]
    for peer in feat_peers():
        term_copy(peer, peer).wait_recv()
    total = terms_recv[0]
    for k in range(1, n_feat):
        total = total + terms_recv[k]
    term[...] = total
    for peer in edge_peers():
        edge_term(peer, e).start()

    relay(1)

    edge_recv[e] = term[...]
    for peer in edge_peers():
        edge_term(peer, peer).wait_recv()
    total = edge_recv[0]
    for k in range(1, n_edge):
        total = total + edge_recv[k]
    total = total * factor
    grad_self_ref[...] = total[:8]
    grad_neigh_ref[...] = total[8:]

    for peer in feat_peers():
        back_copy(peer, peer).wait_recv()
    half_lanes = 4 * lanes
    span = nodes // 2
    for j in range(2):
        for half in range(2):
            at = 2 * half + j
            two(1, 1 - half, j).wait_recv()
            three(1, half, j).wait_recv()
            y_copy(at).wait_recv()
            total = arrived(1, half, j) + y_recv[at].astype(F32)
            for h in range(2):
                for k in range(lanes // span):
                    low = at * lanes + k * span
                    node = h * half_lanes + low
                    src, part = node // nodes, node % nodes // span
                    back = back_recv[src].astype(F32)[part * 8 : part * 8 + 8]
                    out_ref[:, node : node + span] = (
                        total[h * 8 : h * 8 + 8, k * span : (k + 1) * span] + back
                    ).astype(BF16)

    for p in range(2):
        for j in range(2):
            for d in range(2):
                one(p, d, j).wait_send()
                two(p, d, j).wait_send()
                three(p, d, j).wait_send()
    for j in range(4):
        y_copy(j).wait_send()
    for peer in feat_peers():
        node_copy(peer, f).wait_send()
        back_copy(peer, f).wait_send()
        term_copy(peer, f).wait_send()
    for peer in edge_peers():
        edge_term(peer, e).wait_send()


def finish(grad_out, pre_act, w_self, feat_t, agg_t, totals, n_feat, factor):
    nodes, hidden = grad_out.shape
    n_edge, _, half = totals.shape
    features, slab = feat_t.shape
    lanes = half // 4
    vmem = pl.BlockSpec(memory_space=pltpu.VMEM)
    dma = pltpu.SemaphoreType.DMA
    return pl.pallas_call(
        functools.partial(finish_kernel, n_feat, factor),
        in_specs=[vmem] * 5 + [pl.BlockSpec(memory_space=pl.ANY)],
        out_specs=[vmem] * 3,
        out_shape=[
            jax.ShapeDtypeStruct((features, slab), BF16),
            jax.ShapeDtypeStruct((features, hidden), F32),
            jax.ShapeDtypeStruct((features, hidden), F32),
        ],
        scratch_shapes=[
            pltpu.VMEM((nodes, hidden), BF16),
            pltpu.VMEM((n_feat, 16, nodes // 2), BF16),
            pltpu.VMEM((n_feat, 16, nodes // 2), BF16),
            pltpu.VMEM((n_feat, 16, nodes), BF16),
            pltpu.VMEM((n_feat, 16, nodes), BF16),
            pltpu.VMEM((n_feat, 16, hidden), F32),
            pltpu.VMEM((n_feat, 16, hidden), F32),
            pltpu.VMEM((16, hidden), F32),
            pltpu.VMEM((n_edge, 16, hidden), F32),
            pltpu.VMEM((2, 16, half), BF16),
            pltpu.VMEM((2, 2, 16, 2 * lanes), BF16),
            pltpu.VMEM((2, 2, 2, 16, lanes), BF16),
            pltpu.VMEM((2, 2, 2, 16, lanes), BF16),
            pltpu.VMEM((2, 2, 2, 16, lanes), BF16),
            pltpu.VMEM((2, 2, 2, 16, lanes), BF16),
            pltpu.VMEM((4, 16, lanes), BF16),
            pltpu.VMEM((4, 16, lanes), BF16),
            dma((n_feat,)), dma((n_feat,)), dma((n_feat,)), dma((n_feat,)),
            dma((n_feat,)), dma((n_feat,)), dma((n_edge,)), dma((n_edge,)),
            dma((6,)), dma((2, 2, 2)), dma((2, 2, 2)), dma((2, 2, 2)), dma((2, 2, 2)),
            dma((2, 2, 2)), dma((2, 2, 2)), dma((4,)), dma((4,)),
        ],
        compiler_params=pltpu.CompilerParams(
            collective_id=1, has_side_effects=True, vmem_limit_bytes=48 * MIB
        ),
        name="finish",
    )(grad_out, pre_act, w_self, feat_t, agg_t, totals)


def on_device(grad_out, pre_act, feat_t, agg_t, w_self, w_neigh, blocks, row_index, col_index, counts):
    n_feat = lax.axis_size("feat")
    n_edge = lax.axis_size("edge")
    slab_nodes = feat_t.shape[1]
    factor = 1.0 / math.sqrt(slab_nodes * n_edge)
    neigh = send_neigh(grad_out, pre_act, w_neigh, n_feat)
    totals = spread_slots(counts, row_index, col_index, neigh, blocks, n_edge, slab_nodes)
    grad_feat_t, grad_w_self, grad_w_neigh = finish(
        grad_out, pre_act, w_self, feat_t, agg_t, totals, n_feat, factor
    )
    return (grad_feat_t, grad_w_self, grad_w_neigh)


def solution(mesh):
    in_specs = (
        P(("edge", "feat"), None),
        P(("edge", "feat"), None),
        P("feat", "edge"),
        P("feat", "edge"),
        P(),
        P(),
        P("edge", None),
        P("edge"),
        P("edge"),
        P("edge"),
    )
    out_specs = (P("feat", "edge"), P("feat", None), P("feat", None))
    return jax.shard_map(
        on_device, mesh=mesh, in_specs=in_specs, out_specs=out_specs, check_vma=False
    )
```

time: 381 us -> 100 us (0.26)
  waiting for transfers between devices: 146 us -> 0 us
  local copies, waits for them, and re-layouts: 110 us -> 6.08 us
  Pallas kernels: 0 us -> 91.8 us
  other arithmetic: 35.4 us -> 0 us
  blocking collectives: 32.9 us -> 0 us
  matrix products: 30.1 us -> 0 us
  between operations: 16.3 us -> 1.38 us
  starting transfers between devices: 8.22 us -> 0 us
    reduce_scatter x1 -> x0, waiting for transfers between devices: 145 us -> none  [on_device(): lax.psum_scatter(totals.astype(jnp.bfloat16), 'edge', scatter_dimension=0...]
    pallas_call x0 -> x3, Pallas kernels: none -> 91.8 us  [the longest x1 48 us: finish(): pl.pallas_call(functools.partial(finish_kernel, n_feat, factor), in_specs...]
    reshape x5 -> x0, local copies, waits for them, and re-layouts: 51.8 us -> none  [the longest x1 45.9 us: spread_slots(): values = blocks.reshape(slot_count, 64, 64)]
    psum x1 -> x0, blocking collectives: 32.9 us -> none  [on_device(): sum_self, sum_neigh = lax.psum((part_self, part_neigh), 'edge')]
    dot_general x4 -> x0, matrix products: 30.1 us -> none  [the longest x1 18.2 us: spread_slots(): jnp.einsum('sfi,sij->sfj', gathered, values, preferred_element_type=jnp.f...]
    unnamed x16 -> x21, local copies, waits for them, and re-layouts: 27.3 us -> 6.08 us
    scatter-add x1 -> x0, other arithmetic: 17.1 us -> none  [spread_slots(): return totals.at[col_index].add(product)]
    gather x2 -> x0, local copies, waits for them, and re-layouts: 10.1 us -> none  [spread_slots(): jnp.take(node_rows, row_index, axis=0).reshape(slot_count, feat_local, 64)]
  transfers between devices with their start and end apart: 3 -> 0, of which waited for: 1 -> 0; matrix products, arithmetic and copies ran while one was open for 21% -> 0% of each run, Pallas kernels for 0% -> 0%
where the time goes in v1:
time: 100 us; the launch traced here: 99.2 us
  Pallas kernels  91.8 us (92%)
  local copies, waits for them, and re-layouts  6.08 us (6%)
  between operations  1.38 us (1%)
    pallas_call x1, Pallas kernels, finish(): pl.pallas_call(functools.partial(finish_kernel, n_feat, factor), in_specs...  48 us
    pallas_call x1, Pallas kernels, spread_slots(): pl.pallas_call(functools.partial(spread_kernel, per_step), in_specs=[smem...  29.1 us
    pallas_call x1, Pallas kernels, send_neigh(): pl.pallas_call(functools.partial(neigh_kernel, n_feat), in_specs=[pl.Bloc...  14.7 us
    unnamed x21, local copies, waits for them, and re-layouts  6.08 us

profile of v1, /device:TPU:0, one launch (start us, length us, event | category | flops | bytes accessed | tf_op | source)
XLA Modules:
  0.0 99.2 jit_solution(5356635630924305880)
XLA Ops:
  1.3 0.0 copy-start
  1.3 1.2 %copy-done = bf16[2048,256]{1,0:T(8,128)(2,1)S(1)} copy-done((bf16[2048,256]{1,0:T(8,128)(2,1)S(1)}, bf16[2048,256]{1,0:T(8,128)(2,1)}, u32[]{:S(2)}) %copy-start) | copy-done | bytes 1048600
  2.5 0.0 copy-start.2
  2.5 1.2 %copy-done.2 = bf16[2048,256]{1,0:T(8,128)(2,1)S(1)} copy-done((bf16[2048,256]{1,0:T(8,128)(2,1)S(1)}, bf16[2048,256]{1,0:T(8,128)(2,1)}, u32[]{:S(2)}) %copy-start.2) | copy-done | bytes 1048600
  3.7 0.0 copy-start.8
  3.7 0.8 copy-done.8
  4.6 0.0 copy-start.1
  4.6 0.0 copy-start.3
  4.6 0.0 copy-start.5
  4.6 0.0 copy-start.6
  4.6 0.0 copy-start.7
  4.6 14.7 %send_neigh.1.neigh_hbm = bf16[16,16,1024]{2,1,0:T(8,128)(2,1)S(1)} custom-call(bf16[2048,256]{1,0:T(8,128)(2,1)S(1)} %copy-done, bf16[2048,256]{1,0:T(8,128)(2,1)S(1)} %copy-done.2, bf16[128,256]{1,0:T(8,128)(2,1)S(1)} %copy-done.8), custom_call_target="tpu_custom_call" | custom-call | tf_op jit(solution)/shard_map/send_neigh/pallas_call | solution.py:68
  19.3 0.0 copy-start.4
  19.3 0.8 copy-done.4
  20.1 29.1 %spread_slots.1.totals_hbm = bf16[8,16,16384]{2,1,0:T(8,128)(2,1)} custom-call(s32[1]{0:T(128)S(6)} %copy.16.counts_ref, s32[2048]{0:T(1024)} %row_ref.1, s32[2048]{0:T(1024)} %col_ref.1, bf16[16,16,1024]{2,1,0:T(8,128)(2,1)} %copy-done.4, bf16[2048,4096]{1,0:T(8,128)(2,1)} %blocks_hbm.1), custom_call_target="tpu_custom_call" | custom-call | tf_op jit(solution)/shard_map/spread_slots/pallas_call | solution.py:194
  49.2 0.0 copy-done.1
  49.2 0.0 copy-done.3
  49.2 0.0 copy-done.5
  49.2 0.0 copy-done.6
  49.2 0.0 copy-done.7
  49.2 48.0 %finish.1 = (bf16[8,32768]{1,0:T(8,128)(2,1)S(1)}, f32[8,256]{1,0:T(8,128)S(1)}, f32[8,256]{1,0:T(8,128)S(1)}) custom-call(bf16[2048,256]{1,0:T(8,128)(2,1)S(1)} %copy-done.1, bf16[2048,256]{1,0:T(8,128)(2,1)S(1)} %copy-done.3, bf16[128,256]{1,0:T(8,128)(2,1)S(1)} %copy-done.7, bf16[8,32768]{1,0:T(8,128)(2,1)S(1)} %copy-done.5, ...), custom_call_target="tpu_custom_call" | custom-call | tf_op jit(solution)/shard_map/finish/pallas_call | solution.py:449
  97.2 0.8 copy.17
  98.0 0.6 copy.18
  98.6 0.6 copy.19
Async XLA Ops:
  1.3 1.2 %copy-start = (bf16[2048,256]{1,0:T(8,128)(2,1)S(1)}, bf16[2048,256]{1,0:T(8,128)(2,1)}, u32[]{:S(2)}) copy-start(bf16[2048,256]{1,0:T(8,128)(2,1)} %grad_ref.3) | copy-start | bytes 3145732
  2.5 1.2 %copy-start.2 = (bf16[2048,256]{1,0:T(8,128)(2,1)S(1)}, bf16[2048,256]{1,0:T(8,128)(2,1)}, u32[]{:S(2)}) copy-start(bf16[2048,256]{1,0:T(8,128)(2,1)} %pre_ref.3) | copy-start | bytes 3145732
  3.7 0.8 copy-start.8
  4.6 44.6 %copy-start.1 = (bf16[2048,256]{1,0:T(8,128)(2,1)S(1)}, bf16[2048,256]{1,0:T(8,128)(2,1)}, u32[]{:S(2)}) copy-start(bf16[2048,256]{1,0:T(8,128)(2,1)} %grad_ref.3) | copy-start | bytes 3145732
  4.6 44.6 %copy-start.3 = (bf16[2048,256]{1,0:T(8,128)(2,1)S(1)}, bf16[2048,256]{1,0:T(8,128)(2,1)}, u32[]{:S(2)}) copy-start(bf16[2048,256]{1,0:T(8,128)(2,1)} %pre_ref.3) | copy-start | bytes 3145732
  4.6 44.6 %copy-start.5 = (bf16[8,32768]{1,0:T(8,128)(2,1)S(1)}, bf16[8,32768]{1,0:T(8,128)(2,1)}, u32[]{:S(2)}) copy-start(bf16[8,32768]{1,0:T(8,128)(2,1)} %feat_ref.1) | copy-start | bytes 1572868
  4.6 44.6 %copy-start.6 = (bf16[8,32768]{1,0:T(8,128)(2,1)S(1)}, bf16[8,32768]{1,0:T(8,128)(2,1)}, u32[]{:S(2)}) copy-start(bf16[8,32768]{1,0:T(8,128)(2,1)} %agg_ref.1) | copy-start | bytes 1572868
  4.6 44.7 %copy-start.7 = (bf16[128,256]{1,0:T(8,128)(2,1)S(1)}, bf16[128,256]{1,0:T(8,128)(2,1)}, u32[]{:S(2)}) copy-start(bf16[128,256]{1,0:T(8,128)(2,1)} %w_ref.3) | copy-start | bytes 196612
  19.3 0.8 copy-start.4

commit v2 on v0

v2 whole, which is shorter than its diff:
```python
import functools
import math

import jax
import jax.numpy as jnp
from jax import lax
from jax.experimental import pallas as pl
from jax.experimental.pallas import tpu as pltpu
from jax.sharding import PartitionSpec as P

MESH = pl.DeviceIdType.MESH
MIB = 2**20
F32 = jnp.float32
BF16 = jnp.bfloat16
HIGH = dict(preferred_element_type=F32)
NT = (((1,), (1,)), ((), ()))


def masked_rows(grad_ref, pre_ref):
    return jnp.where(pre_ref[...] > 0, grad_ref[...], jnp.zeros_like(grad_ref))


def halves_of(product, owner):
    nodes = product.shape[1]
    rows = product[owner * 8 : owner * 8 + 8]
    both = jnp.concatenate([rows[:, : nodes // 2], rows[:, nodes // 2 :]], 0)
    return both.astype(BF16)


def find_chains(count_ref, col_smem, row_ref, col_ref, row_out, prev_out, last_out):
    slots = row_ref.shape[0] * 128
    count = count_ref[0]

    def count_up(shape):
        return lax.broadcasted_iota(jnp.int32, shape, 0) * 128 + lax.broadcasted_iota(jnp.int32, shape, 1)

    spot = count_up(row_ref.shape)
    alive = spot < count
    row_out[...] = jnp.where(alive, row_ref[...], 0)
    cols = jnp.where(alive, col_ref[...], -2)
    names = count_up(last_out.shape)

    def body(i, carry):
        prev, last = carry
        for u in range(32):
            s = i * 32 + u
            c = jnp.where(s < count, col_smem[s], -1)
            prev = jnp.where((cols == c) & (spot > s), s, prev)
            last = jnp.where(names == c, s, last)
        return prev, last

    none = (jnp.full(row_ref.shape, slots, jnp.int32), jnp.full(last_out.shape, slots, jnp.int32))
    prev, last = lax.fori_loop(0, slots // 32, body, none)
    prev_out[...] = prev
    last_out[...] = last


def build_table(src, neigh, table, permute_ref):
    tiles = neigh.shape[2] // 128
    x = jnp.concatenate([neigh[src, :, t * 128 : (t + 1) * 128] for t in range(tiles)], 0)
    for b in range(2):
        y = jnp.dot(x, permute_ref[:, b * 512 : (b + 1) * 512], **HIGH)
        for t in range(tiles):
            for h in range(2):
                at = t * 16 + h * 8
                both = jnp.concatenate([y[at : at + 8, :256], y[at : at + 8, 256:]], 0)
                table[src * (4 * tiles) + h * 2 * tiles + 2 * t + b] = both.astype(BF16)


def permutation():
    place = lax.broadcasted_iota(jnp.int32, (128, 1024), 1)
    source = place // 512 * 64 + (place % 256) // 8 * 2 + place // 256 % 2
    node = lax.broadcasted_iota(jnp.int32, (128, 1024), 0)
    return jnp.where(source == node, 1.0, 0.0).astype(BF16)


def products(row_smem, prev_smem, blocks, table, sums, even, odd):
    slots = blocks.shape[0]
    steps = slots // 128
    lane = lax.broadcasted_iota(jnp.int32, (8, 128), 1)
    own = lax.broadcasted_iota(jnp.int32, (16, 256), 1) % 8
    sums[slots] = jnp.zeros((8, 128), F32)

    def product(step, g, dst):
        rows = pl.ds(pl.multiple_of(step * 128 + g * 16, 16), 16)
        tiles = [blocks[rows, t * 128 : (t + 1) * 128].astype(F32) for t in range(32)]
        for h in range(2):
            left = []
            for q in range(8):
                mine = table[row_smem[step, g * 16 + h * 8 + q]]
                left.append(jnp.where(own == q, mine, jnp.zeros((16, 256), BF16)))
            right = jnp.concatenate([t[h * 8 : h * 8 + 8] for t in tiles], 0).astype(BF16)
            dst[h * 128 : h * 128 + 128] = jnp.dot(jnp.concatenate(left, 0), right, **HIGH)

    def collect(step, g, src):
        for q in range(16):
            before = sums[prev_smem[step, g * 16 + q]]
            v = jnp.where(lane < 64, src[q * 16 : q * 16 + 8], src[q * 16 + 8 : q * 16 + 16])
            sums[step * 128 + g * 16 + q] = v + before

    kept = (even, odd)
    product(0, 0, even)

    @pl.loop(0, steps)
    def _(step):
        for g in range(8):
            if g < 7:
                product(step, g + 1, kept[(g + 1) % 2])
            else:
                product(jnp.minimum(step + 1, steps - 1), 0, even)
            collect(step, g, kept[g % 2])


def pack(e, last_smem, sums, out_ref):
    half = out_ref.shape[1]
    rows = half // 64 // 128
    lane = lax.broadcasted_iota(jnp.int32, (8, 128), 1)
    for k in range(rows):

        @pl.loop(0, 4)
        def _(v):
            low = pl.multiple_of(k * 8192 + v * 2048, 2048)
            tiles = []
            for u in range(16):
                two = []
                for h in range(2):
                    r = (e * 2 + h) * rows + k
                    a = sums[last_smem[r, v * 32 + 2 * u]]
                    b = sums[last_smem[r, v * 32 + 2 * u + 1]]
                    two.append(jnp.where(lane < 64, a, b) + pltpu.roll(jnp.where(lane < 64, b, a), 64, 1))
                tiles.append(jnp.concatenate(two, 0).astype(BF16))
            out_ref[:, pl.ds(low, 2048)] = jnp.concatenate(tiles, 1)


X_FIRST = 5120
SUBS = ((0, 2048), (2048, 5120))


def layer_kernel(
    n_feat, factor, count_ref, col_smem, index_ref, w_self_ref, w_neigh_ref, grad_hbm, pre_hbm, feat_hbm, agg_hbm,
    blocks_hbm, out_ref, weight_ref,
    grad, pre, feat, agg, blocks, masked, permute, table, sums, even, odd, packed,
    row_v, prev_v, last_v, row_s, prev_s, last_s,
    neigh_send, neigh, back_send, back_recv, node_send, node_recv, terms, terms_recv, term, edge_recv,
    one_recv, two_recv, three_send, three_recv, y_send, y_recv,
    yf_recv, t_sum, t_one, t_two, t_three_send, t_three_recv,
    load_sem, index_sem, neigh_ss, neigh_rs, back_ss, back_rs, node_ss, node_rs, term_ss, term_rs, edge_ss, edge_rs,
    one_ss, one_rs, two_ss, two_rs, three_ss, three_rs, y_ss, y_rs,
    yf_ss, yf_rs, t_one_ss, t_one_rs, t_two_ss, t_two_rs, t_three_ss, t_three_rs,
):
    f = lax.axis_index("feat")
    e = lax.axis_index("edge")
    x, y = e // 2, e % 2
    n_edge = 8
    barrier = pltpu.get_barrier_semaphore()

    @pl.loop(1, n_feat)
    def _(k):
        peer = {"feat": lax.rem(f + k, n_feat)}
        pl.semaphore_signal(barrier, inc=1, device_id=peer, device_id_type=MESH)

    @pl.loop(1, n_edge)
    def _(k):
        peer = {"edge": lax.rem(e + k, n_edge)}
        pl.semaphore_signal(barrier, inc=1, device_id=peer, device_id_type=MESH)

    pairs = ((grad_hbm, grad), (pre_hbm, pre), (feat_hbm, feat), (agg_hbm, agg), (blocks_hbm, blocks))
    loads = [pltpu.make_async_copy(a, b, load_sem.at[i]) for i, (a, b) in enumerate(pairs)]
    for c in loads:
        c.start()

    def to_feat(src, dst, send_sem, recv_sem):
        def copy(peer, slot):
            return pltpu.make_async_remote_copy(
                src_ref=src.at[peer], dst_ref=dst.at[slot], send_sem=send_sem.at[peer], recv_sem=recv_sem.at[slot],
                device_id={"feat": peer}, device_id_type=MESH,
            )

        return copy

    neigh_copy = to_feat(neigh_send, neigh, neigh_ss, neigh_rs)
    back_copy = to_feat(back_send, back_recv, back_ss, back_rs)
    node_copy = to_feat(node_send, node_recv, node_ss, node_rs)
    term_copy = to_feat(terms, terms_recv, term_ss, term_rs)

    def start_all(copy):
        @pl.loop(1, n_feat)
        def _(k):
            copy(lax.rem(f + k, n_feat), f).start()

    def receive_all(copy):
        @pl.loop(1, n_feat)
        def _(k):
            peer = lax.rem(f + k, n_feat)
            copy(peer, peer).wait_recv()

    def sent_all(copy):
        @pl.loop(1, n_feat)
        def _(k):
            copy(lax.rem(f + k, n_feat), f).wait_send()

    loads[0].wait()
    loads[1].wait()
    masked[...] = masked_rows(grad, pre)
    nodes = grad.shape[0]
    product = lax.dot_general(w_neigh_ref[...], masked[...], NT, **HIGH)
    for owner in range(n_feat):
        neigh_send[owner] = halves_of(product, owner)
    pl.semaphore_wait(barrier, n_feat - 1 + n_edge - 1)
    start_all(neigh_copy)

    neigh[f] = neigh_send[f]
    permute[...] = permutation()
    find_chains(count_ref, col_smem, index_ref.at[0], index_ref.at[1], row_v, prev_v, last_v)
    places = ((row_v, row_s), (prev_v, prev_s), (last_v, last_s))
    moves = [pltpu.make_async_copy(a, b, index_sem.at[i]) for i, (a, b) in enumerate(places)]
    for c in moves:
        c.start()
    product = lax.dot_general(w_self_ref[...], masked[...], NT, **HIGH)
    for owner in range(n_feat):
        back_send[owner] = halves_of(product, owner)
    loads[2].wait()
    loads[3].wait()
    for owner in range(n_feat):
        span = slice(owner * nodes, (owner + 1) * nodes)
        both = jnp.concatenate([feat[:, span].astype(F32), agg[:, span].astype(F32)], 0)
        node_send[owner] = both.astype(BF16)
    node_recv[f] = node_send[f]
    back_recv[f] = back_send[f]
    build_table(f, neigh, table, permute)

    @pl.loop(1, n_feat)
    def _(k):
        peer = lax.rem(f + k, n_feat)
        neigh_copy(peer, peer).wait_recv()
        build_table(peer, neigh, table, permute)

    start_all(node_copy)
    start_all(back_copy)
    for c in moves:
        c.wait()
    loads[4].wait()
    products(row_s, prev_s, blocks, table, sums, even, odd)

    half = packed.shape[3] // 2
    step_of = (1, -1)
    OPP, RIGHT, LEFT, OWN = range(4)
    away = {OPP: 2, RIGHT: 1, LEFT: -1, OWN: 0}

    def edge_at(dx, py):
        return lax.rem(x + dx + 4, 4) * 2 + py

    def along_x(src, dst, send_sem, recv_sem, d):
        return pltpu.make_async_remote_copy(
            src_ref=src, dst_ref=dst, send_sem=send_sem, recv_sem=recv_sem,
            device_id={"edge": edge_at(step_of[d], y)}, device_id_type=MESH,
        )

    def along_y(src, dst, send_sem, recv_sem):
        return pltpu.make_async_remote_copy(
            src_ref=src, dst_ref=dst, send_sem=send_sem, recv_sem=recv_sem,
            device_id={"edge": edge_at(0, 1 - y)}, device_id_type=MESH,
        )

    def lanes_of(h, low, high):
        return pl.ds(h * half + low, high - low)

    def sub(j):
        return pl.ds(SUBS[j][0], SUBS[j][1] - SUBS[j][0])

    def one(p, d, j):
        src = packed.at[p, OPP, :, lanes_of(d, *SUBS[j])]
        return along_x(src, one_recv.at[p, d, :, sub(j)], one_ss.at[p, d, j], one_rs.at[p, d, j], d)

    def two(p, d, j):
        src = packed.at[p, RIGHT + d, :, lanes_of(1 - d, *SUBS[j])]
        return along_x(src, two_recv.at[p, d, :, sub(j)], two_ss.at[p, d, j], two_rs.at[p, d, j], d)

    def three(p, d, j):
        return along_x(
            three_send.at[p, d, :, sub(j)], three_recv.at[p, d, :, sub(j)],
            three_ss.at[p, d, j], three_rs.at[p, d, j], d,
        )

    def y_copy(h, j):
        return along_y(y_send.at[h, :, sub(j)], y_recv.at[h, :, sub(j)], y_ss.at[h, j], y_rs.at[h, j])

    def yf_copy(i, h):
        src = packed.at[0, i, :, lanes_of(h, X_FIRST, half)]
        return along_y(src, yf_recv.at[i, h], yf_ss.at[i, h], yf_rs.at[i, h])

    def t_one_copy(d):
        return along_x(t_sum.at[OPP, d], t_one.at[d], t_one_ss.at[d], t_one_rs.at[d], d)

    def t_two_copy(d):
        return along_x(t_sum.at[RIGHT + d, 1 - d], t_two.at[d], t_two_ss.at[d], t_two_rs.at[d], d)

    def t_three_copy(d):
        return along_x(t_three_send.at[d], t_three_recv.at[d], t_three_ss.at[d], t_three_rs.at[d], d)

    both_ways = [(j, d) for j in range(2) for d in range(2)]

    def pack_to(p, i):
        pack(edge_at(away[i], 1 - y if p == 0 else y), last_s, sums, packed.at[p, i])

    pack_to(0, OPP)
    for j, d in both_ways:
        one(0, d, j).start()
    for h in range(2):
        yf_copy(OPP, h).start()
    for d in range(2):
        pack_to(0, RIGHT + d)
        for j in range(2):
            two(0, d, j).start()
        for h in range(2):
            yf_copy(RIGHT + d, h).start()
    pack_to(0, OWN)
    for h in range(2):
        yf_copy(OWN, h).start()
    pack_to(1, OPP)

    def relay(p):
        for j, d in both_ways:
            one(p, d, j).wait_recv()
            low, high = SUBS[j]
            mine = packed[p, RIGHT + d, :, d * half + low : d * half + high].astype(F32)
            three_send[p, d, :, low:high] = (mine + one_recv[p, d, :, low:high].astype(F32)).astype(BF16)
            three(p, d, j).start()

    relay(0)
    for j, d in both_ways:
        one(1, d, j).start()
    for d in range(2):
        pack_to(1, RIGHT + d)
        for j in range(2):
            two(1, d, j).start()
    pack_to(1, OWN)

    receive_all(node_copy)
    stacked = node_recv[...].reshape(n_feat * 16, nodes)
    terms[...] = jnp.dot(stacked, masked[...], **HIGH).reshape(terms.shape)
    start_all(term_copy)
    terms_recv[f] = terms[f]

    def sum_y(i):
        for h in range(2):
            yf_copy(i, h).wait_recv()
            mine = packed[1, i, :, h * half + X_FIRST : (h + 1) * half].astype(F32)
            t_sum[i, h] = (mine + yf_recv[i, h].astype(F32)).astype(BF16)

    sum_y(OPP)
    for d in range(2):
        t_one_copy(d).start()
    for d in range(2):
        sum_y(RIGHT + d)
        t_two_copy(d).start()
    sum_y(OWN)

    def arrived(p, h, low, high):
        return (
            packed[p, OWN, :, h * half + low : h * half + high].astype(F32)
            + three_recv[p, h, :, low:high].astype(F32)
            + two_recv[p, 1 - h, :, low:high].astype(F32)
        )

    for j, h in both_ways:
        two(0, 1 - h, j).wait_recv()
        three(0, h, j).wait_recv()
        y_send[h, :, SUBS[j][0] : SUBS[j][1]] = arrived(0, h, *SUBS[j]).astype(BF16)
        y_copy(h, j).start()

    relay(1)
    for d in range(2):
        t_one_copy(d).wait_recv()
        t_three_send[d] = (t_sum[RIGHT + d, d].astype(F32) + t_one[d].astype(F32)).astype(BF16)
        t_three_copy(d).start()

    receive_all(term_copy)
    total = terms_recv[0]
    for k in range(1, n_feat):
        total = total + terms_recv[k]
    term[...] = total

    def edge_term(peer, slot):
        return pltpu.make_async_remote_copy(
            src_ref=term, dst_ref=edge_recv.at[slot], send_sem=edge_ss.at[peer], recv_sem=edge_rs.at[slot],
            device_id={"edge": peer}, device_id_type=MESH,
        )

    @pl.loop(1, n_edge)
    def _(k):
        edge_term(lax.rem(e + k, n_edge), e).start()

    edge_recv[e] = term[...]
    receive_all(back_copy)

    def finish(h, low, total):
        span = nodes // 2
        for r in range(2):
            for k in range(total.shape[1] // span):
                node = r * 2 * half + h * half + low + k * span
                src, part = node // nodes, node % nodes // span
                back = back_recv[src].astype(F32)[part * 8 : part * 8 + 8]
                rows = total[r * 8 : r * 8 + 8, k * span : (k + 1) * span]
                out_ref[:, node : node + span] = (rows + back).astype(BF16)

    for j, h in both_ways:
        low, high = SUBS[j]
        two(1, 1 - h, j).wait_recv()
        three(1, h, j).wait_recv()
        y_copy(h, j).wait_recv()
        finish(h, low, arrived(1, h, low, high) + y_recv[h, :, low:high].astype(F32))
    for h in range(2):
        t_two_copy(1 - h).wait_recv()
        t_three_copy(h).wait_recv()
        finish(h, X_FIRST, t_sum[OWN, h].astype(F32) + t_three_recv[h].astype(F32) + t_two[1 - h].astype(F32))

    @pl.loop(1, n_edge)
    def _(k):
        peer = lax.rem(e + k, n_edge)
        edge_term(peer, peer).wait_recv()

    total = edge_recv[0]
    for k in range(1, n_edge):
        total = total + edge_recv[k]
    weight_ref[...] = total * factor

    for copy in (neigh_copy, back_copy, node_copy, term_copy):
        sent_all(copy)

    @pl.loop(1, n_edge)
    def _(k):
        edge_term(lax.rem(e + k, n_edge), e).wait_send()

    for p in range(2):
        for j, d in both_ways:
            one(p, d, j).wait_send()
            two(p, d, j).wait_send()
            three(p, d, j).wait_send()
    for j, h in both_ways:
        y_copy(h, j).wait_send()
    for i in range(4):
        for h in range(2):
            yf_copy(i, h).wait_send()
    for d in range(2):
        t_one_copy(d).wait_send()
        t_two_copy(d).wait_send()
        t_three_copy(d).wait_send()


def layer(counts, row_index, col_index, w_self, w_neigh, grad_out, pre_act, feat_t, agg_t, blocks, n_feat, n_edge, factor):
    nodes, hidden = grad_out.shape
    features, slab = feat_t.shape
    slots = blocks.shape[0]
    half = slab // 4
    y_first = half - X_FIRST
    names = n_edge * slab // 64
    index = jnp.stack([row_index, col_index]).reshape(2, slots // 128, 128)
    smem = pl.BlockSpec(memory_space=pltpu.SMEM)
    vmem = pl.BlockSpec(memory_space=pltpu.VMEM)
    hbm = pl.BlockSpec(memory_space=pl.ANY)
    dma = pltpu.SemaphoreType.DMA
    ints = [(slots // 128, 128), (slots // 128, 128), (names // 128, 128)]
    small, large = (n_feat, 16, nodes // 2), (n_feat, 16, nodes)
    x_part = (2, 2, 16, X_FIRST)
    y_part = (2, 16, X_FIRST)
    return pl.pallas_call(
        functools.partial(layer_kernel, n_feat, factor),
        in_specs=[smem, smem, vmem, vmem, vmem] + [hbm] * 5,
        out_specs=[vmem] * 2,
        out_shape=[
            jax.ShapeDtypeStruct((features, slab), BF16),
            jax.ShapeDtypeStruct((2 * features, hidden), F32),
        ],
        scratch_shapes=[
            pltpu.VMEM((nodes, hidden), BF16),
            pltpu.VMEM((nodes, hidden), BF16),
            pltpu.VMEM((features, slab), BF16),
            pltpu.VMEM((features, slab), BF16),
            pltpu.VMEM(blocks.shape, BF16),
            pltpu.VMEM((nodes, hidden), BF16),
            pltpu.VMEM((128, 1024), BF16),
            pltpu.VMEM((slab // 64, 16, 256), BF16),
            pltpu.VMEM((slots + 1, 8, 128), F32),
            pltpu.VMEM((256, 128), F32),
            pltpu.VMEM((256, 128), F32),
            pltpu.VMEM((2, 4, 16, 2 * half), BF16),
            *[pltpu.VMEM(i, jnp.int32) for i in ints],
            *[pltpu.SMEM(i, jnp.int32) for i in ints],
            *[pltpu.VMEM(i, BF16) for i in (small, small, small, small, large, large)],
            pltpu.VMEM((n_feat, 16, hidden), F32),
            pltpu.VMEM((n_feat, 16, hidden), F32),
            pltpu.VMEM((16, hidden), F32),
            pltpu.VMEM((n_edge, 16, hidden), F32),
            *[pltpu.VMEM(i, BF16) for i in (x_part, x_part, x_part, x_part, y_part, y_part)],
            *[pltpu.VMEM((4, 2, 16, y_first), BF16) for i in range(2)],
            *[pltpu.VMEM((2, 16, y_first), BF16) for i in range(4)],
            dma((5,)),
            dma((3,)),
            *[dma((n_feat,)) for i in range(8)],
            dma((n_edge,)),
            dma((n_edge,)),
            *[dma((2, 2, 2)) for i in range(6)],
            dma((2, 2)),
            dma((2, 2)),
            dma((4, 2)),
            dma((4, 2)),
            *[dma((2,)) for i in range(6)],
        ],
        compiler_params=pltpu.CompilerParams(collective_id=0, has_side_effects=True, vmem_limit_bytes=60 * MIB),
        name="layer",
    )(counts, col_index, index, w_self, w_neigh, grad_out, pre_act, feat_t, agg_t, blocks)


def on_device(grad_out, pre_act, feat_t, agg_t, w_self, w_neigh, blocks, row_index, col_index, counts):
    n_feat = lax.axis_size("feat")
    n_edge = lax.axis_size("edge")
    features, slab = feat_t.shape
    factor = 1.0 / math.sqrt(slab * n_edge)
    grad_feat_t, weights = layer(
        counts, row_index, col_index, w_self, w_neigh, grad_out, pre_act, feat_t, agg_t, blocks, n_feat, n_edge, factor
    )
    return (grad_feat_t, weights[:features], weights[features:])


def solution(mesh):
    in_specs = (
        P(("edge", "feat"), None),
        P(("edge", "feat"), None),
        P("feat", "edge"),
        P("feat", "edge"),
        P(),
        P(),
        P("edge", None),
        P("edge"),
        P("edge"),
        P("edge"),
    )
    out_specs = (P("feat", "edge"), P("feat", None), P("feat", None))
    return jax.shard_map(
        on_device, mesh=mesh, in_specs=in_specs, out_specs=out_specs, check_vma=False
    )
```

time: 381 us -> 76.3 us (0.20)
  waiting for transfers between devices: 146 us -> 0 us
  local copies, waits for them, and re-layouts: 110 us -> 3.19 us
  Pallas kernels: 0 us -> 69.6 us
  other arithmetic: 35.4 us -> 1.32 us
  blocking collectives: 32.9 us -> 0 us
  matrix products: 30.1 us -> 0 us
  between operations: 16.3 us -> 1.29 us
  starting transfers between devices: 8.22 us -> 0 us
    reduce_scatter x1 -> x0, waiting for transfers between devices: 145 us -> none  [on_device(): lax.psum_scatter(totals.astype(jnp.bfloat16), 'edge', scatter_dimension=0...]
    pallas_call x0 -> x1, Pallas kernels: none -> 69.6 us  [layer(): pl.pallas_call(functools.partial(layer_kernel, n_feat, factor), in_specs=...]
    reshape x5 -> x0, local copies, waits for them, and re-layouts: 51.8 us -> none  [the longest x1 45.9 us: spread_slots(): values = blocks.reshape(slot_count, 64, 64)]
    psum x1 -> x0, blocking collectives: 32.9 us -> none  [on_device(): sum_self, sum_neigh = lax.psum((part_self, part_neigh), 'edge')]
    dot_general x4 -> x0, matrix products: 30.1 us -> none  [the longest x1 18.2 us: spread_slots(): jnp.einsum('sfi,sij->sfj', gathered, values, preferred_element_type=jnp.f...]
    unnamed x16 -> x1, local copies, waits for them, and re-layouts: 27.3 us -> 1.87 us
    scatter-add x1 -> x0, other arithmetic: 17.1 us -> none  [spread_slots(): return totals.at[col_index].add(product)]
    gather x2 -> x0, local copies, waits for them, and re-layouts: 10.1 us -> none  [spread_slots(): jnp.take(node_rows, row_index, axis=0).reshape(slot_count, feat_local, 64)]
  transfers between devices with their start and end apart: 3 -> 0, of which waited for: 1 -> 0; matrix products, arithmetic and copies ran while one was open for 21% -> 0% of each run, Pallas kernels for 0% -> 0%
where the time goes in v2:
time: 76.3 us; the launch traced here: 75.4 us
  Pallas kernels  69.6 us (91%)
  local copies, waits for them, and re-layouts  3.19 us (4%)
  other arithmetic  1.32 us (2%)
  between operations  1.29 us (2%)
    pallas_call x1, Pallas kernels, layer(): pl.pallas_call(functools.partial(layer_kernel, n_feat, factor), in_specs=...  69.6 us
    unnamed x1, local copies, waits for them, and re-layouts  1.87 us

profile of v2, /device:TPU:0, one launch (start us, length us, event | category | flops | bytes accessed | tf_op | source)
XLA Modules:
  0.0 75.4 jit_solution(3409831432474972490)
XLA Ops:
  1.3 1.3 %pad_add_fusion.index_ref = s32[2,16,128]{2,1,0:T(8,128)} fusion(s32[1,16,128]{2,1,0:T(8,128)} %bitcast.2, s32[1,16,128]{2,1,0:T(8,128)} %bitcast.3), kind=kLoop, calls=%fused_computation | loop fusion | flops 4096 | bytes 32768 | tf_op jit(solution)/shard_map/stack | solution.py:458
  2.6 69.6 %layer.1 = (bf16[8,32768]{1,0:T(8,128)(2,1)}, f32[16,256]{1,0:T(8,128)}) custom-call(s32[1]{0:T(128)S(6)} %copy.14.count_ref, s32[2048]{0:T(1024)} %col_smem.1, s32[2,16,128]{2,1,0:T(8,128)} %pad_add_fusion.index_ref, bf16[128,256]{1,0:T(8,128)(2,1)} %w_self_ref.1, bf16[128,256]{1,0:T(8,128)(2,1)} %w_neigh_ref.1, bf16[2048,256]{1,0:T(8,128)(2,1)} %grad_hbm.1, ...), custom_call_target="tpu_custom_call" | custom-call | tf_op jit(solution)/shard_map/layer/pallas_call | solution.py:467
  72.2 1.3 %fusion = (f32[8,256]{1,0:T(8,128)}, f32[8,256]{1,0:T(8,128)}) fusion(f32[16,256]{1,0:T(8,128)} %get-tuple-element.6), kind=kLoop, calls=%fused_computation.1 | loop fusion | bytes 32768 | tf_op jit(solution)/shard_map/slice | solution.py:523
  73.5 1.9 %copy.15 = bf16[8,32768]{1,0:T(8,128)(2,1)} copy(bf16[8,32768]{1,0:T(8,128)(2,1)} %get-tuple-element.12) | data formatting | bytes 1048576

commit v3 on v2

--- a/solution.py
+++ b/solution.py
@@ -37,34 +37,37 @@
     spot = count_up(row_ref.shape)
     alive = spot < count
     row_out[...] = jnp.where(alive, row_ref[...], 0)
-    cols = jnp.where(alive, col_ref[...], -2)
-    names = count_up(last_out.shape)
+    cols = [jnp.where(alive & (spot % 2 == k), col_ref[...], -2) for k in range(2)]
+    names = count_up(last_out.shape[1:])
 
     def body(i, carry):
-        prev, last = carry
+        prev, last = carry[0], list(carry[1:])
         for u in range(32):
             s = i * 32 + u
+            place = i * 16 + u // 2
             c = jnp.where(s < count, col_smem[s], -1)
-            prev = jnp.where((cols == c) & (spot > s), s, prev)
-            last = jnp.where(names == c, s, last)
-        return prev, last
-
-    none = (jnp.full(row_ref.shape, slots, jnp.int32), jnp.full(last_out.shape, slots, jnp.int32))
-    prev, last = lax.fori_loop(0, slots // 32, body, none)
+            prev = jnp.where((cols[u % 2] == c) & (spot > s), place, prev)
+            last[u % 2] = jnp.where(names == c, place, last[u % 2])
+        return prev, *last
+
+    none = [jnp.full(n, slots // 2, jnp.int32) for n in (row_ref.shape, names.shape, names.shape)]
+    prev, *last = lax.fori_loop(0, slots // 32, body, tuple(none))
     prev_out[...] = prev
-    last_out[...] = last
-
-
-def build_table(src, neigh, table, permute_ref):
+    for k in range(2):
+        last_out[k] = last[k]
+
+
+def build_table(sources, neigh, table, permute_ref):
     tiles = neigh.shape[2] // 128
-    x = jnp.concatenate([neigh[src, :, t * 128 : (t + 1) * 128] for t in range(tiles)], 0)
+    x = jnp.concatenate([neigh[i, :, t * 128 : (t + 1) * 128] for i in sources for t in range(tiles)], 0)
     for b in range(2):
         y = jnp.dot(x, permute_ref[:, b * 512 : (b + 1) * 512], **HIGH)
-        for t in range(tiles):
-            for h in range(2):
-                at = t * 16 + h * 8
-                both = jnp.concatenate([y[at : at + 8, :256], y[at : at + 8, 256:]], 0)
-                table[src * (4 * tiles) + h * 2 * tiles + 2 * t + b] = both.astype(BF16)
+        for n, i in enumerate(sources):
+            for t in range(tiles):
+                for h in range(2):
+                    at = (n * tiles + t) * 16 + h * 8
+                    both = jnp.concatenate([y[at : at + 8, :256], y[at : at + 8, 256:]], 0)
+                    table[i * (4 * tiles) + h * 2 * tiles + 2 * t + b] = both.astype(BF16)
 
 
 def permutation():
@@ -79,7 +82,8 @@
     steps = slots // 128
     lane = lax.broadcasted_iota(jnp.int32, (8, 128), 1)
     own = lax.broadcasted_iota(jnp.int32, (16, 256), 1) % 8
-    sums[slots] = jnp.zeros((8, 128), F32)
+    for k in range(2):
+        sums[k][slots // 2] = jnp.zeros((8, 128), F32)
 
     def product(step, g, dst):
         rows = pl.ds(pl.multiple_of(step * 128 + g * 16, 16), 16)
@@ -94,9 +98,9 @@
 
     def collect(step, g, src):
         for q in range(16):
-            before = sums[prev_smem[step, g * 16 + q]]
+            before = sums[q % 2][prev_smem[step, g * 16 + q]]
             v = jnp.where(lane < 64, src[q * 16 : q * 16 + 8], src[q * 16 + 8 : q * 16 + 16])
-            sums[step * 128 + g * 16 + q] = v + before
+            sums[q % 2][step * 64 + g * 8 + q // 2] = v + before
 
     kept = (even, odd)
     product(0, 0, even)
@@ -125,8 +129,10 @@
                 two = []
                 for h in range(2):
                     r = (e * 2 + h) * rows + k
-                    a = sums[last_smem[r, v * 32 + 2 * u]]
-                    b = sums[last_smem[r, v * 32 + 2 * u + 1]]
+                    a, b = [
+                        sums[0][last_smem[0, r, v * 32 + 2 * u + w]] + sums[1][last_smem[1, r, v * 32 + 2 * u + w]]
+                        for w in range(2)
+                    ]
                     two.append(jnp.where(lane < 64, a, b) + pltpu.roll(jnp.where(lane < 64, b, a), 64, 1))
                 tiles.append(jnp.concatenate(two, 0).astype(BF16))
             out_ref[:, pl.ds(low, 2048)] = jnp.concatenate(tiles, 1)
@@ -137,9 +143,9 @@
 
 
 def layer_kernel(
-    n_feat, factor, count_ref, col_smem, index_ref, w_self_ref, w_neigh_ref, grad_hbm, pre_hbm, feat_hbm, agg_hbm,
+    n_feat, factor, count_ref, col_smem, row_hbm, col_hbm, w_self_hbm, w_neigh_hbm, grad_hbm, pre_hbm, feat_hbm, agg_hbm,
     blocks_hbm, out_ref, weight_ref,
-    grad, pre, feat, agg, blocks, masked, permute, table, sums, even, odd, packed,
+    w_neigh, grad, pre, row, col, w_self, feat, agg, blocks, masked, permute, table, sums_even, sums_odd, even, odd, packed,
     row_v, prev_v, last_v, row_s, prev_s, last_s,
     neigh_send, neigh, back_send, back_recv, node_send, node_recv, terms, terms_recv, term, edge_recv,
     one_recv, two_recv, three_send, three_recv, y_send, y_recv,
@@ -152,6 +158,7 @@
     e = lax.axis_index("edge")
     x, y = e // 2, e % 2
     n_edge = 8
+    sums = (sums_even, sums_odd)
     barrier = pltpu.get_barrier_semaphore()
 
     @pl.loop(1, n_feat)
@@ -164,9 +171,12 @@
         peer = {"edge": lax.rem(e + k, n_edge)}
         pl.semaphore_signal(barrier, inc=1, device_id=peer, device_id_type=MESH)
 
-    pairs = ((grad_hbm, grad), (pre_hbm, pre), (feat_hbm, feat), (agg_hbm, agg), (blocks_hbm, blocks))
+    pairs = (
+        (w_neigh_hbm, w_neigh), (grad_hbm, grad), (pre_hbm, pre), (row_hbm, row), (col_hbm, col),
+        (w_self_hbm, w_self), (feat_hbm, feat), (agg_hbm, agg), (blocks_hbm, blocks),
+    )
     loads = [pltpu.make_async_copy(a, b, load_sem.at[i]) for i, (a, b) in enumerate(pairs)]
-    for c in loads:
+    for c in loads[:3]:
         c.start()
 
     def to_feat(src, dst, send_sem, recv_sem):
@@ -199,11 +209,13 @@
         def _(k):
             copy(lax.rem(f + k, n_feat), f).wait_send()
 
-    loads[0].wait()
-    loads[1].wait()
+    for c in loads[:3]:
+        c.wait()
+    for c in loads[3:]:
+        c.start()
     masked[...] = masked_rows(grad, pre)
     nodes = grad.shape[0]
-    product = lax.dot_general(w_neigh_ref[...], masked[...], NT, **HIGH)
+    product = lax.dot_general(w_neigh[...], masked[...], NT, **HIGH)
     for owner in range(n_feat):
         neigh_send[owner] = halves_of(product, owner)
     pl.semaphore_wait(barrier, n_feat - 1 + n_edge - 1)
@@ -211,35 +223,37 @@
 
     neigh[f] = neigh_send[f]
     permute[...] = permutation()
-    find_chains(count_ref, col_smem, index_ref.at[0], index_ref.at[1], row_v, prev_v, last_v)
+    loads[3].wait()
+    loads[4].wait()
+    find_chains(count_ref, col_smem, row, col, row_v, prev_v, last_v)
     places = ((row_v, row_s), (prev_v, prev_s), (last_v, last_s))
     moves = [pltpu.make_async_copy(a, b, index_sem.at[i]) for i, (a, b) in enumerate(places)]
     for c in moves:
         c.start()
-    product = lax.dot_general(w_self_ref[...], masked[...], NT, **HIGH)
+    loads[5].wait()
+    product = lax.dot_general(w_self[...], masked[...], NT, **HIGH)
     for owner in range(n_feat):
         back_send[owner] = halves_of(product, owner)
-    loads[2].wait()
-    loads[3].wait()
+    loads[6].wait()
+    loads[7].wait()
     for owner in range(n_feat):
         span = slice(owner * nodes, (owner + 1) * nodes)
         both = jnp.concatenate([feat[:, span].astype(F32), agg[:, span].astype(F32)], 0)
         node_send[owner] = both.astype(BF16)
     node_recv[f] = node_send[f]
     back_recv[f] = back_send[f]
-    build_table(f, neigh, table, permute)
-
-    @pl.loop(1, n_feat)
-    def _(k):
-        peer = lax.rem(f + k, n_feat)
-        neigh_copy(peer, peer).wait_recv()
-        build_table(peer, neigh, table, permute)
-
+    sent_all(neigh_copy)
     start_all(node_copy)
     start_all(back_copy)
+    for low in range(0, n_feat, 4):
+        sources = [lax.rem(f + k, n_feat) for k in range(low, low + 4)]
+        for k in range(low, low + 4):
+            if k > 0:
+                neigh_copy(sources[k - low], sources[k - low]).wait_recv()
+        build_table(sources, neigh, table, permute)
     for c in moves:
         c.wait()
-    loads[4].wait()
+    loads[8].wait()
     products(row_s, prev_s, blocks, table, sums, even, odd)
 
     half = packed.shape[3] // 2
@@ -425,7 +439,7 @@
         total = total + edge_recv[k]
     weight_ref[...] = total * factor
 
-    for copy in (neigh_copy, back_copy, node_copy, term_copy):
+    for copy in (back_copy, node_copy, term_copy):
         sent_all(copy)
 
     @pl.loop(1, n_edge)
@@ -455,33 +469,38 @@
     half = slab // 4
     y_first = half - X_FIRST
     names = n_edge * slab // 64
-    index = jnp.stack([row_index, col_index]).reshape(2, slots // 128, 128)
+    spots = (slots // 128, 128)
     smem = pl.BlockSpec(memory_space=pltpu.SMEM)
     vmem = pl.BlockSpec(memory_space=pltpu.VMEM)
     hbm = pl.BlockSpec(memory_space=pl.ANY)
     dma = pltpu.SemaphoreType.DMA
-    ints = [(slots // 128, 128), (slots // 128, 128), (names // 128, 128)]
+    ints = [spots, spots, (2, names // 128, 128)]
     small, large = (n_feat, 16, nodes // 2), (n_feat, 16, nodes)
     x_part = (2, 2, 16, X_FIRST)
     y_part = (2, 16, X_FIRST)
     return pl.pallas_call(
         functools.partial(layer_kernel, n_feat, factor),
-        in_specs=[smem, smem, vmem, vmem, vmem] + [hbm] * 5,
+        in_specs=[smem, smem] + [hbm] * 9,
         out_specs=[vmem] * 2,
         out_shape=[
             jax.ShapeDtypeStruct((features, slab), BF16),
             jax.ShapeDtypeStruct((2 * features, hidden), F32),
         ],
         scratch_shapes=[
+            pltpu.VMEM(w_neigh.shape, BF16),
             pltpu.VMEM((nodes, hidden), BF16),
             pltpu.VMEM((nodes, hidden), BF16),
+            pltpu.VMEM(spots, jnp.int32),
+            pltpu.VMEM(spots, jnp.int32),
+            pltpu.VMEM(w_self.shape, BF16),
             pltpu.VMEM((features, slab), BF16),
             pltpu.VMEM((features, slab), BF16),
             pltpu.VMEM(blocks.shape, BF16),
             pltpu.VMEM((nodes, hidden), BF16),
             pltpu.VMEM((128, 1024), BF16),
             pltpu.VMEM((slab // 64, 16, 256), BF16),
-            pltpu.VMEM((slots + 1, 8, 128), F32),
+            pltpu.VMEM((slots // 2 + 1, 8, 128), F32),
+            pltpu.VMEM((slots // 2 + 1, 8, 128), F32),
             pltpu.VMEM((256, 128), F32),
             pltpu.VMEM((256, 128), F32),
             pltpu.VMEM((2, 4, 16, 2 * half), BF16),
@@ -495,7 +514,7 @@
             *[pltpu.VMEM(i, BF16) for i in (x_part, x_part, x_part, x_part, y_part, y_part)],
             *[pltpu.VMEM((4, 2, 16, y_first), BF16) for i in range(2)],
             *[pltpu.VMEM((2, 16, y_first), BF16) for i in range(4)],
-            dma((5,)),
+            dma((9,)),
             dma((3,)),
             *[dma((n_feat,)) for i in range(8)],
             dma((n_edge,)),
@@ -509,18 +528,38 @@
         ],
         compiler_params=pltpu.CompilerParams(collective_id=0, has_side_effects=True, vmem_limit_bytes=60 * MIB),
         name="layer",
-    )(counts, col_index, index, w_self, w_neigh, grad_out, pre_act, feat_t, agg_t, blocks)
+    )(counts, col_index, row_index.reshape(spots), col_index.reshape(spots), w_self, w_neigh, grad_out, pre_act, feat_t, agg_t, blocks)
+
+
+def split_kernel(out_ref, weight_ref, feat_ref, self_ref, neigh_ref):
+    features = out_ref.shape[0]
+    feat_ref[...] = out_ref[...]
+    self_ref[...] = weight_ref[:features]
+    neigh_ref[...] = weight_ref[features:]
+
+
+def split(out, weights):
+    features = out.shape[0]
+    weight = jax.ShapeDtypeStruct((features, weights.shape[1]), F32)
+    vmem = pl.BlockSpec(memory_space=pltpu.VMEM)
+    return pl.pallas_call(
+        split_kernel,
+        in_specs=[vmem] * 2,
+        out_specs=[vmem] * 3,
+        out_shape=[jax.ShapeDtypeStruct(out.shape, BF16), weight, weight],
+        name="split",
+    )(out, weights)
 
 
 def on_device(grad_out, pre_act, feat_t, agg_t, w_self, w_neigh, blocks, row_index, col_index, counts):
     n_feat = lax.axis_size("feat")
     n_edge = lax.axis_size("edge")
-    features, slab = feat_t.shape
+    slab = feat_t.shape[1]
     factor = 1.0 / math.sqrt(slab * n_edge)
-    grad_feat_t, weights = layer(
+    out, weights = layer(
         counts, row_index, col_index, w_self, w_neigh, grad_out, pre_act, feat_t, agg_t, blocks, n_feat, n_edge, factor
     )
-    return (grad_feat_t, weights[:features], weights[features:])
+    return tuple(split(out, weights))
 
 
 def solution(mesh):

time: 76.3 us -> 69.4 us (0.910)
  local copies, waits for them, and re-layouts: 3.19 us -> 0 us
  Pallas kernels: 69.6 us -> 67.6 us
  other arithmetic: 1.32 us -> 0 us
    pallas_call x1, Pallas kernels: 69.6 us -> 65.7 us  [layer(): pl.pallas_call(functools.partial(layer_kernel, n_feat, factor), in_specs=...]
    pallas_call x0 -> x1, Pallas kernels: none -> 1.88 us  [split(): pl.pallas_call(split_kernel, in_specs=[vmem] * 2, out_specs=[vmem] * 3, o...]
    unnamed x1 -> x0, local copies, waits for them, and re-layouts: 1.87 us -> none
    another operation x1 -> x0, other arithmetic: 1.32 us -> none  [layer(): index = jnp.stack([row_index, col_index]).reshape(2, slots // 128, 128)]
    slice x1 -> x0, local copies, waits for them, and re-layouts: 1.32 us -> none  [on_device(): return (grad_feat_t, weights[:features], weights[features:])]
where the time goes in v3:
time: 69.4 us; the launch traced here: 68.9 us
  Pallas kernels  67.6 us (97%)
  between operations  1.29 us (2%)
    pallas_call x1, Pallas kernels, layer(): pl.pallas_call(functools.partial(layer_kernel, n_feat, factor), in_specs=...  65.7 us
    pallas_call x1, Pallas kernels, split(): pl.pallas_call(split_kernel, in_specs=[vmem] * 2, out_specs=[vmem] * 3, o...  1.88 us

profile of v3, /device:TPU:0, one launch (start us, length us, event | category | flops | bytes accessed | tf_op | source)
XLA Modules:
  0.0 68.9 jit_solution(111497126480670936)
XLA Ops:
  1.3 65.7 %layer.1 = (bf16[8,32768]{1,0:T(8,128)(2,1)}, f32[16,256]{1,0:T(8,128)}) custom-call(s32[1]{0:T(128)S(6)} %copy.13.count_ref, s32[2048]{0:T(1024)} %col_smem.1, s32[16,128]{1,0:T(8,128)} %bitcast.3, s32[16,128]{1,0:T(8,128)} %bitcast.2, bf16[128,256]{1,0:T(8,128)(2,1)} %w_self_hbm.1, bf16[128,256]{1,0:T(8,128)(2,1)} %w_neigh_hbm.1, ...), custom_call_target="tpu_custom_call" | custom-call | tf_op jit(solution)/shard_map/layer/pallas_call | solution.py:481
  67.0 1.9 %split.1 = (bf16[8,32768]{1,0:T(8,128)(2,1)}, f32[8,256]{1,0:T(8,128)}, f32[8,256]{1,0:T(8,128)}) custom-call(bf16[8,32768]{1,0:T(8,128)(2,1)} %get-tuple-element.5.out_ref, f32[16,256]{1,0:T(8,128)} %get-tuple-element.6.weight_ref), custom_call_target="tpu_custom_call" | custom-call | tf_op jit(solution)/shard_map/split/pallas_call | solution.py:545

commit v4 on v3

--- a/solution.py
+++ b/solution.py
@@ -116,26 +116,17 @@
 
 
 def pack(e, last_smem, sums, out_ref):
-    half = out_ref.shape[1]
-    rows = half // 64 // 128
+    rows = out_ref.shape[1] // 64 // 128
     lane = lax.broadcasted_iota(jnp.int32, (8, 128), 1)
     for k in range(rows):
-
-        @pl.loop(0, 4)
-        def _(v):
-            low = pl.multiple_of(k * 8192 + v * 2048, 2048)
-            tiles = []
-            for u in range(16):
-                two = []
-                for h in range(2):
-                    r = (e * 2 + h) * rows + k
-                    a, b = [
-                        sums[0][last_smem[0, r, v * 32 + 2 * u + w]] + sums[1][last_smem[1, r, v * 32 + 2 * u + w]]
-                        for w in range(2)
-                    ]
-                    two.append(jnp.where(lane < 64, a, b) + pltpu.roll(jnp.where(lane < 64, b, a), 64, 1))
-                tiles.append(jnp.concatenate(two, 0).astype(BF16))
-            out_ref[:, pl.ds(low, 2048)] = jnp.concatenate(tiles, 1)
+        for u in range(64):
+            two = []
+            for h in range(2):
+                r = (e * 2 + h) * rows + k
+                a, b = [sums[0][last_smem[0, r, c]] + sums[1][last_smem[1, r, c]] for c in (2 * u, 2 * u + 1)]
+                two.append(jnp.where(lane < 64, a, b) + pltpu.roll(jnp.where(lane < 64, b, a), 64, 1))
+            low = (k * 64 + u) * 128
+            out_ref[:, low : low + 128] = jnp.concatenate(two, 0).astype(BF16)
 
 
 X_FIRST = 5120
@@ -179,35 +170,20 @@
     for c in loads[:3]:
         c.start()
 
-    def to_feat(src, dst, send_sem, recv_sem):
-        def copy(peer, slot):
-            return pltpu.make_async_remote_copy(
-                src_ref=src.at[peer], dst_ref=dst.at[slot], send_sem=send_sem.at[peer], recv_sem=recv_sem.at[slot],
-                device_id={"feat": peer}, device_id_type=MESH,
-            )
-
-        return copy
-
-    neigh_copy = to_feat(neigh_send, neigh, neigh_ss, neigh_rs)
-    back_copy = to_feat(back_send, back_recv, back_ss, back_rs)
-    node_copy = to_feat(node_send, node_recv, node_ss, node_rs)
-    term_copy = to_feat(terms, terms_recv, term_ss, term_rs)
-
-    def start_all(copy):
-        @pl.loop(1, n_feat)
-        def _(k):
-            copy(lax.rem(f + k, n_feat), f).start()
-
-    def receive_all(copy):
+    def all_of(ref, sem):
+        return pltpu.make_async_copy(ref, ref, sem)
+
+    def start_all(src, dst, send_sem, recv_sem):
         @pl.loop(1, n_feat)
         def _(k):
             peer = lax.rem(f + k, n_feat)
-            copy(peer, peer).wait_recv()
-
-    def sent_all(copy):
-        @pl.loop(1, n_feat)
-        def _(k):
-            copy(lax.rem(f + k, n_feat), f).wait_send()
+            pltpu.make_async_remote_copy(
+                src_ref=src.at[peer], dst_ref=dst.at[f], send_sem=send_sem, recv_sem=recv_sem,
+                device_id={"feat": peer}, device_id_type=MESH,
+            ).start()
+
+    def await_all(ref, sem):
+        all_of(ref.at[pl.ds(0, n_feat - 1)], sem).wait()
 
     for c in loads[:3]:
         c.wait()
@@ -219,7 +195,7 @@
     for owner in range(n_feat):
         neigh_send[owner] = halves_of(product, owner)
     pl.semaphore_wait(barrier, n_feat - 1 + n_edge - 1)
-    start_all(neigh_copy)
+    start_all(neigh_send, neigh, neigh_ss, neigh_rs)
 
     neigh[f] = neigh_send[f]
     permute[...] = permutation()
@@ -242,14 +218,12 @@
         node_send[owner] = both.astype(BF16)
     node_recv[f] = node_send[f]
     back_recv[f] = back_send[f]
-    sent_all(neigh_copy)
-    start_all(node_copy)
-    start_all(back_copy)
+    await_all(neigh_send, neigh_ss)
+    start_all(node_send, node_recv, node_ss, node_rs)
+    start_all(back_send, back_recv, back_ss, back_rs)
+    await_all(neigh, neigh_rs)
     for low in range(0, n_feat, 4):
         sources = [lax.rem(f + k, n_feat) for k in range(low, low + 4)]
-        for k in range(low, low + 4):
-            if k > 0:
-                neigh_copy(sources[k - low], sources[k - low]).wait_recv()
         build_table(sources, neigh, table, permute)
     for c in moves:
         c.wait()
@@ -259,7 +233,6 @@
     half = packed.shape[3] // 2
     step_of = (1, -1)
     OPP, RIGHT, LEFT, OWN = range(4)
-    away = {OPP: 2, RIGHT: 1, LEFT: -1, OWN: 0}
 
     def edge_at(dx, py):
         return lax.rem(x + dx + 4, 4) * 2 + py
@@ -284,54 +257,62 @@
 
     def one(p, d, j):
         src = packed.at[p, OPP, :, lanes_of(d, *SUBS[j])]
-        return along_x(src, one_recv.at[p, d, :, sub(j)], one_ss.at[p, d, j], one_rs.at[p, d, j], d)
+        return along_x(src, one_recv.at[p, d, :, sub(j)], one_ss, one_rs.at[p, d, j], d)
 
     def two(p, d, j):
         src = packed.at[p, RIGHT + d, :, lanes_of(1 - d, *SUBS[j])]
-        return along_x(src, two_recv.at[p, d, :, sub(j)], two_ss.at[p, d, j], two_rs.at[p, d, j], d)
+        return along_x(src, two_recv.at[p, d, :, sub(j)], two_ss, two_rs.at[p, d, j], d)
 
     def three(p, d, j):
         return along_x(
             three_send.at[p, d, :, sub(j)], three_recv.at[p, d, :, sub(j)],
-            three_ss.at[p, d, j], three_rs.at[p, d, j], d,
+            three_ss, three_rs.at[p, d, j], d,
         )
 
     def y_copy(h, j):
-        return along_y(y_send.at[h, :, sub(j)], y_recv.at[h, :, sub(j)], y_ss.at[h, j], y_rs.at[h, j])
+        return along_y(y_send.at[h, :, sub(j)], y_recv.at[h, :, sub(j)], y_ss, y_rs.at[h, j])
 
     def yf_copy(i, h):
         src = packed.at[0, i, :, lanes_of(h, X_FIRST, half)]
-        return along_y(src, yf_recv.at[i, h], yf_ss.at[i, h], yf_rs.at[i, h])
+        return along_y(src, yf_recv.at[i, h], yf_ss, yf_rs.at[i])
 
     def t_one_copy(d):
-        return along_x(t_sum.at[OPP, d], t_one.at[d], t_one_ss.at[d], t_one_rs.at[d], d)
+        return along_x(t_sum.at[OPP, d], t_one.at[d], t_one_ss, t_one_rs.at[d], d)
 
     def t_two_copy(d):
-        return along_x(t_sum.at[RIGHT + d, 1 - d], t_two.at[d], t_two_ss.at[d], t_two_rs.at[d], d)
+        return along_x(t_sum.at[RIGHT + d, 1 - d], t_two.at[d], t_two_ss, t_two_rs.at[d], d)
 
     def t_three_copy(d):
-        return along_x(t_three_send.at[d], t_three_recv.at[d], t_three_ss.at[d], t_three_rs.at[d], d)
+        return along_x(t_three_send.at[d], t_three_recv.at[d], t_three_ss, t_three_rs.at[d], d)
 
     both_ways = [(j, d) for j in range(2) for d in range(2)]
 
-    def pack_to(p, i):
-        pack(edge_at(away[i], 1 - y if p == 0 else y), last_s, sums, packed.at[p, i])
-
-    pack_to(0, OPP)
-    for j, d in both_ways:
-        one(0, d, j).start()
-    for h in range(2):
-        yf_copy(OPP, h).start()
-    for d in range(2):
-        pack_to(0, RIGHT + d)
-        for j in range(2):
-            two(0, d, j).start()
-        for h in range(2):
-            yf_copy(RIGHT + d, h).start()
-    pack_to(0, OWN)
-    for h in range(2):
-        yf_copy(OWN, h).start()
-    pack_to(1, OPP)
+    def pack_to(t):
+        p, i = t // 4, t % 4
+        dx = lax.rem(2 + 3 * i + (i // 2) * (3 + 2 * (i % 2)), 4)
+        py = (1 - p) * (1 - y) + p * y
+        pack(lax.rem(x + dx, 4) * 2 + py, last_s, sums, packed.at[p, i])
+
+    @pl.loop(0, 5)
+    def _(t):
+        pack_to(t)
+
+        @pl.when(t == OPP)
+        def _():
+            for j, d in both_ways:
+                one(0, d, j).start()
+
+        for d in range(2):
+
+            @pl.when(t == RIGHT + d)
+            def _():
+                for j in range(2):
+                    two(0, d, j).start()
+
+        @pl.when(t < 4)
+        def _():
+            for h in range(2):
+                yf_copy(t, h).start()
 
     def relay(p):
         for j, d in both_ways:
@@ -344,21 +325,27 @@
     relay(0)
     for j, d in both_ways:
         one(1, d, j).start()
-    for d in range(2):
-        pack_to(1, RIGHT + d)
-        for j in range(2):
-            two(1, d, j).start()
-    pack_to(1, OWN)
-
-    receive_all(node_copy)
+
+    @pl.loop(5, 8)
+    def _(t):
+        pack_to(t)
+        for d in range(2):
+
+            @pl.when(t == 4 + RIGHT + d)
+            def _():
+                for j in range(2):
+                    two(1, d, j).start()
+
+
+    await_all(node_recv, node_rs)
     stacked = node_recv[...].reshape(n_feat * 16, nodes)
     terms[...] = jnp.dot(stacked, masked[...], **HIGH).reshape(terms.shape)
-    start_all(term_copy)
+    start_all(terms, terms_recv, term_ss, term_rs)
     terms_recv[f] = terms[f]
 
     def sum_y(i):
+        all_of(yf_recv.at[i], yf_rs.at[i]).wait()
         for h in range(2):
-            yf_copy(i, h).wait_recv()
             mine = packed[1, i, :, h * half + X_FIRST : (h + 1) * half].astype(F32)
             t_sum[i, h] = (mine + yf_recv[i, h].astype(F32)).astype(BF16)
 
@@ -389,24 +376,22 @@
         t_three_send[d] = (t_sum[RIGHT + d, d].astype(F32) + t_one[d].astype(F32)).astype(BF16)
         t_three_copy(d).start()
 
-    receive_all(term_copy)
+    await_all(terms_recv, term_rs)
     total = terms_recv[0]
     for k in range(1, n_feat):
         total = total + terms_recv[k]
     term[...] = total
 
-    def edge_term(peer, slot):
-        return pltpu.make_async_remote_copy(
-            src_ref=term, dst_ref=edge_recv.at[slot], send_sem=edge_ss.at[peer], recv_sem=edge_rs.at[slot],
-            device_id={"edge": peer}, device_id_type=MESH,
-        )
-
     @pl.loop(1, n_edge)
     def _(k):
-        edge_term(lax.rem(e + k, n_edge), e).start()
+        peer = lax.rem(e + k, n_edge)
+        pltpu.make_async_remote_copy(
+            src_ref=term, dst_ref=edge_recv.at[e], send_sem=edge_ss, recv_sem=edge_rs,
+            device_id={"edge": peer}, device_id_type=MESH,
+        ).start()
 
     edge_recv[e] = term[...]
-    receive_all(back_copy)
+    await_all(back_recv, back_rs)
 
     def finish(h, low, total):
         span = nodes // 2
@@ -429,37 +414,23 @@
         t_three_copy(h).wait_recv()
         finish(h, X_FIRST, t_sum[OWN, h].astype(F32) + t_three_recv[h].astype(F32) + t_two[1 - h].astype(F32))
 
-    @pl.loop(1, n_edge)
-    def _(k):
-        peer = lax.rem(e + k, n_edge)
-        edge_term(peer, peer).wait_recv()
-
+    edge_bytes = edge_recv.at[pl.ds(0, n_edge - 1)]
+    all_of(edge_bytes, edge_rs).wait()
     total = edge_recv[0]
     for k in range(1, n_edge):
         total = total + edge_recv[k]
     weight_ref[...] = total * factor
 
-    for copy in (back_copy, node_copy, term_copy):
-        sent_all(copy)
-
-    @pl.loop(1, n_edge)
-    def _(k):
-        edge_term(lax.rem(e + k, n_edge), e).wait_send()
-
-    for p in range(2):
-        for j, d in both_ways:
-            one(p, d, j).wait_send()
-            two(p, d, j).wait_send()
-            three(p, d, j).wait_send()
-    for j, h in both_ways:
-        y_copy(h, j).wait_send()
-    for i in range(4):
-        for h in range(2):
-            yf_copy(i, h).wait_send()
-    for d in range(2):
-        t_one_copy(d).wait_send()
-        t_two_copy(d).wait_send()
-        t_three_copy(d).wait_send()
+    await_all(back_send, back_ss)
+    await_all(node_send, node_ss)
+    await_all(terms, term_ss)
+
+    sent = (
+        (edge_bytes, edge_ss), (one_recv, one_ss), (two_recv, two_ss), (three_send, three_ss), (y_send, y_ss),
+        (yf_recv, yf_ss), (t_one, t_one_ss), (t_two, t_two_ss), (t_three_send, t_three_ss),
+    )
+    for ref, sem in sent:
+        all_of(ref, sem).wait()
 
 
 def layer(counts, row_index, col_index, w_self, w_neigh, grad_out, pre_act, feat_t, agg_t, blocks, n_feat, n_edge, factor):
@@ -516,15 +487,11 @@
             *[pltpu.VMEM((2, 16, y_first), BF16) for i in range(4)],
             dma((9,)),
             dma((3,)),
-            *[dma((n_feat,)) for i in range(8)],
-            dma((n_edge,)),
-            dma((n_edge,)),
-            *[dma((2, 2, 2)) for i in range(6)],
-            dma((2, 2)),
-            dma((2, 2)),
-            dma((4, 2)),
-            dma((4, 2)),
-            *[dma((2,)) for i in range(6)],
+            *[dma] * 10,
+            *[dma, dma((2, 2, 2))] * 3,
+            *[dma, dma((2, 2))],
+            *[dma, dma((4,))],
+            *[dma, dma((2,))] * 3,
         ],
         compiler_params=pltpu.CompilerParams(collective_id=0, has_side_effects=True, vmem_limit_bytes=60 * MIB),
         name="layer",

time: 69.4 us -> 65.6 us (0.945)
  Pallas kernels: 67.6 us -> 64.1 us
    pallas_call x1, Pallas kernels: 65.7 us -> 62.2 us  [layer(): pl.pallas_call(functools.partial(layer_kernel, n_feat, factor), in_specs=...]
where the time goes in v4:
time: 65.6 us; the launch traced here: 65.3 us
  Pallas kernels  64.1 us (98%)
  between operations  1.29 us (2%)
    pallas_call x1, Pallas kernels, layer(): pl.pallas_call(functools.partial(layer_kernel, n_feat, factor), in_specs=...  62.2 us
    pallas_call x1, Pallas kernels, split(): pl.pallas_call(split_kernel, in_specs=[vmem] * 2, out_specs=[vmem] * 3, o...  1.88 us

profile of v4, /device:TPU:0, one launch (start us, length us, event | category | flops | bytes accessed | tf_op | source)
XLA Modules:
  0.0 65.3 jit_solution(1324817174875778041)
XLA Ops:
  1.3 62.2 %layer.1 = (bf16[8,32768]{1,0:T(8,128)(2,1)}, f32[16,256]{1,0:T(8,128)}) custom-call(s32[1]{0:T(128)S(6)} %copy.13.count_ref, s32[2048]{0:T(1024)} %col_smem.1, s32[16,128]{1,0:T(8,128)} %bitcast.3, s32[16,128]{1,0:T(8,128)} %bitcast.2, bf16[128,256]{1,0:T(8,128)(2,1)} %w_self_hbm.1, bf16[128,256]{1,0:T(8,128)(2,1)} %w_neigh_hbm.1, ...), custom_call_target="tpu_custom_call" | custom-call | tf_op jit(solution)/shard_map/layer/pallas_call | solution.py:452
  63.5 1.9 %split.1 = (bf16[8,32768]{1,0:T(8,128)(2,1)}, f32[8,256]{1,0:T(8,128)}, f32[8,256]{1,0:T(8,128)}) custom-call(bf16[8,32768]{1,0:T(8,128)(2,1)} %get-tuple-element.5.out_ref, f32[16,256]{1,0:T(8,128)} %get-tuple-element.6.weight_ref), custom_call_target="tpu_custom_call" | custom-call | tf_op jit(solution)/shard_map/split/pallas_call | solution.py:512

commit v5 on v4

--- a/solution.py
+++ b/solution.py
@@ -129,8 +129,8 @@
             out_ref[:, low : low + 128] = jnp.concatenate(two, 0).astype(BF16)
 
 
-X_FIRST = 5120
-SUBS = ((0, 2048), (2048, 5120))
+X_FIRST = 5632
+SUBS = ((0, 2560), (2560, 5632))
 
 
 def layer_kernel(
@@ -337,17 +337,26 @@
                     two(1, d, j).start()
 
 
+    def sum_y(i):
+        all_of(yf_recv.at[i], yf_rs.at[i]).wait()
+        for h in range(2):
+            mine = packed[1, i, :, h * half + X_FIRST : (h + 1) * half].astype(F32)
+            t_sum[i, h] = (mine + yf_recv[i, h].astype(F32)).astype(BF16)
+
+    def arrived(p, h, low, high):
+        return (
+            packed[p, OWN, :, h * half + low : h * half + high].astype(F32)
+            + three_recv[p, h, :, low:high].astype(F32)
+            + two_recv[p, 1 - h, :, low:high].astype(F32)
+        )
+
     await_all(node_recv, node_rs)
     stacked = node_recv[...].reshape(n_feat * 16, nodes)
     terms[...] = jnp.dot(stacked, masked[...], **HIGH).reshape(terms.shape)
     start_all(terms, terms_recv, term_ss, term_rs)
     terms_recv[f] = terms[f]
 
-    def sum_y(i):
-        all_of(yf_recv.at[i], yf_rs.at[i]).wait()
-        for h in range(2):
-            mine = packed[1, i, :, h * half + X_FIRST : (h + 1) * half].astype(F32)
-            t_sum[i, h] = (mine + yf_recv[i, h].astype(F32)).astype(BF16)
+    relay(1)
 
     sum_y(OPP)
     for d in range(2):
@@ -355,22 +364,11 @@
     for d in range(2):
         sum_y(RIGHT + d)
         t_two_copy(d).start()
-    sum_y(OWN)
-
-    def arrived(p, h, low, high):
-        return (
-            packed[p, OWN, :, h * half + low : h * half + high].astype(F32)
-            + three_recv[p, h, :, low:high].astype(F32)
-            + two_recv[p, 1 - h, :, low:high].astype(F32)
-        )
-
     for j, h in both_ways:
         two(0, 1 - h, j).wait_recv()
         three(0, h, j).wait_recv()
         y_send[h, :, SUBS[j][0] : SUBS[j][1]] = arrived(0, h, *SUBS[j]).astype(BF16)
         y_copy(h, j).start()
-
-    relay(1)
     for d in range(2):
         t_one_copy(d).wait_recv()
         t_three_send[d] = (t_sum[RIGHT + d, d].astype(F32) + t_one[d].astype(F32)).astype(BF16)
@@ -394,14 +392,14 @@
     await_all(back_recv, back_rs)
 
     def finish(h, low, total):
-        span = nodes // 2
+        span, piece = nodes // 2, 512
         for r in range(2):
-            for k in range(total.shape[1] // span):
-                node = r * 2 * half + h * half + low + k * span
-                src, part = node // nodes, node % nodes // span
-                back = back_recv[src].astype(F32)[part * 8 : part * 8 + 8]
-                rows = total[r * 8 : r * 8 + 8, k * span : (k + 1) * span]
-                out_ref[:, node : node + span] = (rows + back).astype(BF16)
+            for k in range(total.shape[1] // piece):
+                node = r * 2 * half + h * half + low + k * piece
+                src, part, at = node // nodes, node % nodes // span, node % span
+                back = back_recv[src, :, at : at + piece].astype(F32)[part * 8 : part * 8 + 8]
+                rows = total[r * 8 : r * 8 + 8, k * piece : (k + 1) * piece]
+                out_ref[:, node : node + piece] = (rows + back).astype(BF16)
 
     for j, h in both_ways:
         low, high = SUBS[j]
@@ -409,6 +407,7 @@
         three(1, h, j).wait_recv()
         y_copy(h, j).wait_recv()
         finish(h, low, arrived(1, h, low, high) + y_recv[h, :, low:high].astype(F32))
+    sum_y(OWN)
     for h in range(2):
         t_two_copy(1 - h).wait_recv()
         t_three_copy(h).wait_recv()

time: 65.6 us -> 64.9 us (0.989)
  Pallas kernels: 64.1 us -> 63.4 us
    pallas_call x1, Pallas kernels: 62.2 us -> 61.5 us  [layer(): pl.pallas_call(functools.partial(layer_kernel, n_feat, factor), in_specs=...]
where the time goes in v5:
time: 64.9 us; the launch traced here: 64.6 us
  Pallas kernels  63.4 us (98%)
  between operations  1.29 us (2%)
    pallas_call x1, Pallas kernels, layer(): pl.pallas_call(functools.partial(layer_kernel, n_feat, factor), in_specs=...  61.5 us
    pallas_call x1, Pallas kernels, split(): pl.pallas_call(split_kernel, in_specs=[vmem] * 2, out_specs=[vmem] * 3, o...  1.88 us

profile of v5, /device:TPU:0, one launch (start us, length us, event | category | flops | bytes accessed | tf_op | source)
XLA Modules:
  0.0 64.6 jit_solution(2344739120837932828)
XLA Ops:
  1.3 61.5 %layer.1 = (bf16[8,32768]{1,0:T(8,128)(2,1)}, f32[16,256]{1,0:T(8,128)}) custom-call(s32[1]{0:T(128)S(6)} %copy.13.count_ref, s32[2048]{0:T(1024)} %col_smem.1, s32[16,128]{1,0:T(8,128)} %bitcast.3, s32[16,128]{1,0:T(8,128)} %bitcast.2, bf16[128,256]{1,0:T(8,128)(2,1)} %w_self_hbm.1, bf16[128,256]{1,0:T(8,128)(2,1)} %w_neigh_hbm.1, ...), custom_call_target="tpu_custom_call" | custom-call | tf_op jit(solution)/shard_map/layer/pallas_call | solution.py:451
  62.8 1.9 %split.1 = (bf16[8,32768]{1,0:T(8,128)(2,1)}, f32[8,256]{1,0:T(8,128)}, f32[8,256]{1,0:T(8,128)}) custom-call(bf16[8,32768]{1,0:T(8,128)(2,1)} %get-tuple-element.5.out_ref, f32[16,256]{1,0:T(8,128)} %get-tuple-element.6.weight_ref), custom_call_target="tpu_custom_call" | custom-call | tf_op jit(solution)/shard_map/split/pallas_call | solution.py:511

commit v6 on v5

--- a/solution.py
+++ b/solution.py
@@ -105,7 +105,7 @@
     kept = (even, odd)
     product(0, 0, even)
 
-    @pl.loop(0, steps)
+    @pl.loop(0, steps, unroll=2)
     def _(step):
         for g in range(8):
             if g < 7:

time: 64.9 us -> 63.7 us (0.982)
  Pallas kernels: 63.4 us -> 62.2 us
    pallas_call x1, Pallas kernels: 61.5 us -> 60.4 us  [layer(): pl.pallas_call(functools.partial(layer_kernel, n_feat, factor), in_specs=...]
where the time goes in v6:
time: 63.7 us; the launch traced here: 63.5 us
  Pallas kernels  62.2 us (98%)
  between operations  1.29 us (2%)
    pallas_call x1, Pallas kernels, layer(): pl.pallas_call(functools.partial(layer_kernel, n_feat, factor), in_specs=...  60.4 us
    pallas_call x1, Pallas kernels, split(): pl.pallas_call(split_kernel, in_specs=[vmem] * 2, out_specs=[vmem] * 3, o...  1.88 us

profile of v6, /device:TPU:0, one launch (start us, length us, event | category | flops | bytes accessed | tf_op | source)
XLA Modules:
  0.0 63.5 jit_solution(9956853613214704256)
XLA Ops:
  1.3 60.4 %layer.1 = (bf16[8,32768]{1,0:T(8,128)(2,1)}, f32[16,256]{1,0:T(8,128)}) custom-call(s32[1]{0:T(128)S(6)} %copy.13.count_ref, s32[2048]{0:T(1024)} %col_smem.1, s32[16,128]{1,0:T(8,128)} %bitcast.3, s32[16,128]{1,0:T(8,128)} %bitcast.2, bf16[128,256]{1,0:T(8,128)(2,1)} %w_self_hbm.1, bf16[128,256]{1,0:T(8,128)(2,1)} %w_neigh_hbm.1, ...), custom_call_target="tpu_custom_call" | custom-call | tf_op jit(solution)/shard_map/layer/pallas_call | solution.py:451
  61.6 1.9 %split.1 = (bf16[8,32768]{1,0:T(8,128)(2,1)}, f32[8,256]{1,0:T(8,128)}, f32[8,256]{1,0:T(8,128)}) custom-call(bf16[8,32768]{1,0:T(8,128)(2,1)} %get-tuple-element.5.out_ref, f32[16,256]{1,0:T(8,128)} %get-tuple-element.6.weight_ref), custom_call_target="tpu_custom_call" | custom-call | tf_op jit(solution)/shard_map/split/pallas_call | solution.py:511
